TPU v7x, 32 devices: a whole 2x2x4 slice. The times are simulated.
32 devices in a mesh: samp: 4 (over z), seq: 8 (over y, x, core).
Axes of the slice: x: 2, y: 2, z: 4, core: 2. Of those that a mesh axis runs over, the one named last changes fastest.
Arguments:
- atom_input: bfloat16 [32, 4096, 128], P('samp', 'seq'), may hold values from -6 to 6
- token_input: bfloat16 [32, 512, 768], P('samp', 'seq'), may hold values from -6 to 6
- atom_counts: int32 [512], replicated, may hold values from 1 to 8
- key_offsets: int32 [128], P('seq'), may hold values from -96 to 0, as said below
- atom_pairs: bfloat16 [128, 32, 128, 16], P('seq'), may hold values from -6 to 6
- pair_features: bfloat16 [512, 512, 128], P('seq'), may hold values from -6 to 6
- single_features: bfloat16 [512, 384], P('seq'), may hold values from -6 to 6
- noise_levels: float32 [32], P('samp'), may hold values from 0.5 to 160
- noise_direction: float32 [384], replicated, may hold values from -6 to 6
- atom_proj: bfloat16 [128, 512], P('samp'), may hold values from -0.5 to 0.5
- atom_qbias: bfloat16 [128], P('samp'), may hold values from -4 to 4
- atom_pairw: bfloat16 [16, 4], P('samp'), may hold values from -1.5 to 1.5
- atom_outw: bfloat16 [128, 128], P('samp'), may hold values from -1 to 1
- atom_upw: bfloat16 [128, 512], P('samp'), may hold values from -0.5 to 0.5
- atom_downw: bfloat16 [256, 128], P('samp'), may hold values from -0.375 to 0.375
- pool_weight: bfloat16 [128, 768], P('samp'), may hold values from -0.5 to 0.5
- cond_weight: bfloat16 [384, 4608], P('samp'), may hold values from -0.3125 to 0.3125
- cond_bias: bfloat16 [4608], P('samp'), may hold values from -4 to 4
- token_proj: bfloat16 [768, 3072], P('samp'), may hold values from -0.21875 to 0.21875
- token_qbias: bfloat16 [768], P('samp'), may hold values from -4 to 4
- token_pairw: bfloat16 [128, 16], P('samp'), may hold values from -0.5 to 0.5
- token_outw: bfloat16 [768, 768], P('samp'), may hold values from -0.875 to 0.875
- token_upw: bfloat16 [768, 3072], P('samp'), may hold values from -0.21875 to 0.21875
- token_downw: bfloat16 [1536, 768], P('samp'), may hold values from -0.15625 to 0.15625
- cotangent: bfloat16 [32, 512, 768], P('samp', 'seq'), may hold values from -6 to 6
Outputs:
- block_out: bfloat16 [32, 512, 768], P('samp', 'seq')
- atom_grad: float32 [32, 4096, 128], P('samp', 'seq')
- token_grad: float32 [32, 512, 768], P('samp', 'seq')
- grad_atom_proj: float32 [128, 512], P('samp')
- grad_atom_qbias: float32 [128], P('samp')
- grad_atom_pairw: float32 [16, 4], P('samp')
- grad_atom_outw: float32 [128, 128], P('samp')
- grad_atom_upw: float32 [128, 512], P('samp')
- grad_atom_downw: float32 [256, 128], P('samp')
- grad_pool_weight: float32 [128, 768], P('samp')
- grad_cond_weight: float32 [384, 4608], P('samp')
- grad_cond_bias: float32 [4608], P('samp')
- grad_token_proj: float32 [768, 3072], P('samp')
- grad_token_qbias: float32 [768], P('samp')
- grad_token_pairw: float32 [128, 16], P('samp')
- grad_token_outw: float32 [768, 768], P('samp')
- grad_token_upw: float32 [768, 3072], P('samp')
- grad_token_downw: float32 [1536, 768], P('samp')
Inputs may be any that keep to these rules, and one draw needn't show every extreme that they name: `key_offsets`: both ends of the range occur.
All inputs are finite; a program needn't handle non-finite values.
Results may differ from a plain program's by a relative error of at most 0.03.
Values may be sent and summed in bfloat16 or wider, within the bound.
A program may use at most 384 MiB of HBM per device.

v0:
```python
import functools

import jax
import jax.numpy as jnp
from jax import lax
from jax.experimental import pallas as pl
from jax.experimental.pallas import tpu as pltpu
from jax.sharding import PartitionSpec as P

MAX_ATOMS = 8
WIN_Q = 32
WIN_K = 128
ATOM_HEADS = 4
RIM = 96
LANES = 128

norm_eps = 1e-05
sigma_data = 16.0
masked_score = -1000000000.0
bf16 = jnp.bfloat16
f32 = jnp.float32
vmem_bytes = 56 << 20


def dot_last(left_op, right_op):
    return jnp.einsum("...k,kn->...n", left_op, right_op, preferred_element_type=f32)


def dot_back(grad_op, weight):
    return jnp.einsum("...n,kn->...k", grad_op, weight, preferred_element_type=f32)


def weight_grad(left_op, grad_op):
    flat_left = left_op.reshape(-1, left_op.shape[-1])
    flat_grad = grad_op.reshape(-1, grad_op.shape[-1])
    return jnp.einsum("rk,rn->kn", flat_left, flat_grad, preferred_element_type=f32)


def mm(left_op, right_op):
    return lax.dot_general(left_op, right_op, (((1,), (0,)), ((), ())), preferred_element_type=f32)


def mm_nt(left_op, right_op):
    return lax.dot_general(left_op, right_op, (((1,), (1,)), ((), ())), preferred_element_type=f32)


def mm_tn(left_op, right_op):
    return lax.dot_general(left_op, right_op, (((0,), (0,)), ((), ())), preferred_element_type=f32)


def norm_stats(operand):
    center = operand - jnp.mean(operand, -1, keepdims=True)
    inv_std = lax.rsqrt(jnp.mean(center * center, -1, keepdims=True) + norm_eps)
    return (center * inv_std, inv_std)


def norm_back(normed, inv_std, grad_op):
    return inv_std * (
        grad_op
        - jnp.mean(grad_op, -1, keepdims=True)
        - normed * jnp.mean(grad_op * normed, -1, keepdims=True)
    )


def sigmoid(operand):
    return 1.0 / (1.0 + jnp.exp(-operand))


def whole(shape):
    return pl.BlockSpec(shape, lambda *_: (0,) * len(shape))


def per_sample(shape):
    return pl.BlockSpec((1,) + shape, lambda b, *_: (b,) + (0,) * len(shape))


def params():
    return pltpu.CompilerParams(vmem_limit_bytes=vmem_bytes)


def square_sums(ones_op, squares):
    upper = squares.astype(bf16)
    lower = (squares - upper.astype(f32)).astype(bf16)
    return upper, lower


def head_masks(count, width, heads, head_dim, first):
    row = lax.broadcasted_iota(jnp.int32, (heads * count, width), 0)
    lane = lax.broadcasted_iota(jnp.int32, (heads * count, width), 1)
    inside = (lane - first) // head_dim == row // count
    return jnp.where(inside & (lane >= first), 1.0, 0.0).astype(bf16)


def head_stack(rows, heads, head_dim, first, masks=None):
    if masks is None:
        masks = head_masks(rows.shape[0], rows.shape[1], heads, head_dim, first)
    return jnp.concatenate([rows] * heads, 0) * masks


def head_fold(stacked, heads, head_dim, first):
    count = stacked.shape[0] // heads
    lane = lax.broadcasted_iota(jnp.int32, (count, stacked.shape[1]), 1)
    total = jnp.zeros((count, stacked.shape[1]), f32)
    for head in range(heads):
        low = first + head * head_dim
        part = stacked[head * count : (head + 1) * count]
        total = jnp.where((lane >= low) & (lane < low + head_dim), part, total)
    return total


MESH = pl.DeviceIdType.MESH


def places():
    samp_pos, seq_pos = lax.axis_index("samp"), lax.axis_index("seq")
    core, across, along = seq_pos % 2, seq_pos // 2 % 2, seq_pos // 4

    def index(along, across, core):
        return (along * 2 + across) * 2 + core

    return (
        samp_pos,
        seq_pos,
        index(along, across, 1 - core),
        index(along, 1 - across, core),
        index(1 - along, across, core),
        index(1 - along, 1 - across, core),
    )


def remote(source, target, send_sem, recv_sem, device):
    return pltpu.make_async_remote_copy(
        src_ref=source,
        dst_ref=target,
        send_sem=send_sem,
        recv_sem=recv_sem,
        device_id=device,
        device_id_type=MESH,
    )


def greet(devices):
    barrier = pltpu.get_barrier_semaphore()
    for device in devices:
        pl.semaphore_signal(barrier, inc=1, device_id=device, device_id_type=MESH)
    pl.semaphore_wait(barrier, len(devices))


def pick(position, values):
    chosen = values[0]
    for index, value in enumerate(values[1:], 1):
        chosen = jnp.where(position == index, value, chosen)
    return chosen


class WeightGather:
    def __init__(self, shapes, samp, seq):
        self.shapes, self.samp, self.seq = shapes, samp, seq
        self.splits = [self.split(shape, seq) for shape in shapes]

    @staticmethod
    def split(shape, parts):
        rows, columns = shape
        for down in (1, 2, 4, 8):
            across = parts // down
            if rows % (16 * down) == 0 and columns % (LANES * across) == 0:
                return (down, across)
        return None

    @staticmethod
    def fits(shapes, samp, seq):
        return (
            samp == 4
            and seq == 8
            and len(shapes) == 5
            and all(WeightGather.split(shape, seq) for shape in shapes)
        )

    def full_shapes(self):
        return [(rows * self.samp, columns) for rows, columns in self.shapes]

    def scratch(self):
        count = len(self.shapes)
        return [
            pltpu.SemaphoreType.DMA((9, self.samp, count)),
            pltpu.SemaphoreType.DMA((8, self.samp, count)),
            pltpu.SemaphoreType.DMA((2, count)),
        ] + [pltpu.VMEM(shape, bf16) for shape in self.shapes]

    def params(self):
        return pltpu.CompilerParams(
            vmem_limit_bytes=vmem_bytes, collective_id=1, has_side_effects=True
        )

    def cell(self, ref, weight, origin, part):
        rows, columns = self.shapes[weight]
        down, across = self.splits[weight]
        height, width = rows // down, columns // across
        low = origin * rows + part // across * height
        left = part % across * width
        return ref.at[
            pl.ds(pl.multiple_of(low, 16), height), pl.ds(pl.multiple_of(left, LANES), width)
        ]

    def origin(self, position, turn):
        order = [sorted(range(self.samp), key=lambda o: (abs(o - z), o)) for z in range(self.samp)]
        if isinstance(turn, int):
            return pick(position, [order[z][turn] for z in range(self.samp)])
        return pick(
            position, [pick(turn, [order[z][t] for t in range(self.samp)]) for z in range(self.samp)]
        )

    def own_copies(self, shards, fulls, own, held, stage):
        z = places()[0]
        copies = []
        for w, shard in enumerate(shards):
            rows = self.shapes[w][0]
            target = fulls[w].at[pl.ds(pl.multiple_of(z * rows, 16), rows), :]
            ends = (shard, held[w]) if stage == 0 else (held[w], target)
            copies.append(pltpu.make_async_copy(*ends, own.at[stage, w]))
        return copies

    def start(self, shards, fulls, send, recv, own, held):
        z, me, sib, xn, yn, dg = places()
        above, below = lax.rem(z + 1, self.samp), lax.rem(z + self.samp - 1, self.samp)
        greet([(z, sib), (z, xn), (z, yn), (above, me), (below, me)])
        for w, shard in enumerate(shards):
            source = self.cell(shard, w, 0, me)
            target = self.cell(fulls[w], w, z, me)

            @pl.when(z < self.samp - 1)
            def _():
                remote(source, target, send.at[0, 0, w], recv.at[0, z, w], (z + 1, me)).start()

            @pl.when(z > 0)
            def _():
                remote(source, target, send.at[1, 0, w], recv.at[0, z, w], (z - 1, me)).start()

        for copy in self.own_copies(shards, fulls, own, held, 0):
            copy.start()

    def place_own(self, shards, fulls, own, held):
        for copy in self.own_copies(shards, fulls, own, held, 0):
            copy.wait()
        for copy in self.own_copies(shards, fulls, own, held, 1):
            copy.start()

    def share_own(self, turn, origin, sources, fulls, send, recv):
        z, me, sib, xn, yn, dg = places()
        for kind, part in ((2, xn), (3, yn), (5, sib)):
            for w, source in enumerate(sources):
                target = self.cell(fulls[w], w, origin, me)
                arrival = {2: 1, 3: 2, 5: 4}[kind]
                remote(
                    source, target, send.at[kind, turn, w], recv.at[arrival, origin, w], (z, part)
                ).start()

    def wait_cell(self, fulls, recv, kind, w, origin, part, device):
        target = self.cell(fulls[w], w, origin, part)
        remote(target, target, recv.at[kind, origin, w], recv.at[kind, origin, w], device).wait_recv()

    def issue(self, turn, fulls, send, recv):
        z, me, sib, xn, yn, dg = places()
        origin = self.origin(z, turn)
        count = len(self.shapes)
        for w in range(count):
            self.wait_cell(fulls, recv, 0, w, origin, me, (z, sib))
        for w in range(count):
            cell = self.cell(fulls[w], w, origin, me)

            @pl.when((origin < z) & (z < self.samp - 1))
            def _():
                remote(cell, cell, send.at[0, turn, w], recv.at[0, origin, w], (z + 1, me)).start()

            @pl.when((origin > z) & (z > 0))
            def _():
                remote(cell, cell, send.at[1, turn, w], recv.at[0, origin, w], (z - 1, me)).start()

        cells = [self.cell(fulls[w], w, origin, me) for w in range(count)]
        self.share_own(turn, origin, cells, fulls, send, recv)

    def passed_on(self, w):
        return w in (0, 3)

    def finish(self, turn, fulls, send, recv):
        z, me, sib, xn, yn, dg = places()
        origin = self.origin(z, turn)
        count = len(self.shapes)
        for kind, part, other, by in ((1, xn, yn, True), (2, yn, xn, False)):
            for w in range(count):
                self.wait_cell(fulls, recv, kind, w, origin, part, (z, part))
                cell = self.cell(fulls[w], w, origin, part)
                if self.passed_on(w) == by:
                    remote(
                        cell, cell, send.at[4, turn, w], recv.at[3, origin, w], (z, other)
                    ).start()
                remote(
                    cell, cell, send.at[5 + kind, turn, w], recv.at[4 + kind, origin, w], (z, sib)
                ).start()

    def diagonal(self, turn, fulls, send, recv):
        z, me, sib, xn, yn, dg = places()
        origin = self.origin(z, turn)
        for w in range(len(self.shapes)):
            self.wait_cell(fulls, recv, 3, w, origin, dg, (z, yn))
            cell = self.cell(fulls[w], w, origin, dg)
            remote(cell, cell, send.at[8, turn, w], recv.at[7, origin, w], (z, sib)).start()

    def drain(self, shards, fulls, send, recv, own, held):
        z, me, sib, xn, yn, dg = places()
        count = len(self.shapes)

        def sent(kind, turn, w):
            cell = self.cell(fulls[w], w, 0, me)
            remote(cell, cell, send.at[kind, turn, w], recv.at[0, 0, w], (z, sib)).wait_send()

        def one(turn, carry):
            origin = self.origin(z, turn)
            for w in range(count):
                for kind in range(2, 9):
                    sent(kind, turn, w)

                @pl.when((z < self.samp - 1) & (origin < z))
                def _():
                    sent(0, turn, w)

                @pl.when((z > 0) & (origin > z))
                def _():
                    sent(1, turn, w)

                for kind in range(4, 8):
                    self.wait_cell(fulls, recv, kind, w, origin, sib, (z, sib))
            return carry

        lax.fori_loop(1, self.samp, one, 0)
        for w in range(count):

            @pl.when(z < self.samp - 1)
            def _():
                sent(0, 0, w)

            @pl.when(z > 0)
            def _():
                sent(1, 0, w)

        for copy in self.own_copies(shards, fulls, own, held, 1):
            copy.wait()

    def step(self, sample, shards, fulls, send, recv, own, *held):
        @pl.when(sample == 0)
        def _():
            self.start(shards, fulls, send, recv, own, held)

        @pl.when(sample == 1)
        def _():
            self.place_own(shards, fulls, own, held)

        for at, turn in ((2, 1), (3, 2), (5, 3)):

            @pl.when(sample == at)
            def _():
                self.issue(turn, fulls, send, recv)

        for at, turn in ((4, 1), (5, 2), (7, 3)):

            @pl.when(sample == at)
            def _():
                self.finish(turn, fulls, send, recv)

        for at, turn in ((5, 1), (7, 2)):

            @pl.when(sample == at)
            def _():
                self.diagonal(turn, fulls, send, recv)

    def last(self, sample, shards, fulls, send, recv, own, *held):
        @pl.when(sample == pl.num_programs(0) - 1)
        def _():
            self.diagonal(3, fulls, send, recv)
            self.drain(shards, fulls, send, recv, own, held)


def edge_kernel(
    samp,
    seq,
    proj_ref,
    upw_ref,
    pool_ref,
    outw_ref,
    down_ref,
    tiny_ref,
    rows_ref,
    wide_out,
    down_out,
    tiny_out,
    ext_out,
    held,
    send,
    recv,
):
    z, me = lax.axis_index("samp"), lax.axis_index("seq")
    sib = places()[2]
    core = me % 2
    samples, slots, width = rows_ref.shape
    right, left = lax.rem(me + 1, seq), lax.rem(me + seq - 1, seq)
    others = [lax.rem(z + hop, samp) for hop in range(1, samp)]
    greet([(other, me) for other in others] + [(z, sib), (z, right), (z, left)])
    low = 0
    for ref in (proj_ref, upw_ref, pool_ref, outw_ref):
        held[:, low : low + ref.shape[1]] = ref[...]
        low += ref.shape[1]

    def half(out, origin, part):
        rows = out.shape[0] // samp
        first = origin * rows + part * (rows // 2)
        return out.at[pl.ds(pl.multiple_of(first, 16), rows // 2), :]

    def own_half(ref):
        rows = ref.shape[0]
        return ref.at[pl.ds(pl.multiple_of(core * (rows // 2), 16), rows // 2), :]

    def tiny_place(origin):
        rows = tiny_ref.shape[0]
        return tiny_out.at[pl.ds(pl.multiple_of(origin * rows, 16), rows), :]

    copies = []
    for hop, other in enumerate(others):
        device = (other, me)
        copies.append(
            [
                remote(own_half(held), half(wide_out, z, core), send.at[0, hop], recv.at[0, hop], device),
                remote(own_half(down_ref), half(down_out, z, core), send.at[1, hop], recv.at[1, hop], device),
                remote(tiny_ref, tiny_place(z), send.at[2, hop], recv.at[2, hop], device),
            ]
        )
    for group in copies:
        for copy in group:
            copy.start()
    before, after = ext_out.at[:, :RIM, :], ext_out.at[:, RIM + slots :, :]
    to_right = remote(rows_ref.at[:, slots - RIM :, :], before, send.at[5, 0], recv.at[5, 0], (z, right))
    to_left = remote(rows_ref.at[:, :RIM, :], after, send.at[5, 1], recv.at[5, 1], (z, left))
    first, last = me == 0, me == seq - 1

    @pl.when(~last)
    def _():
        to_right.start()

    @pl.when(~first)
    def _():
        to_left.start()

    @pl.when(first)
    def _():
        ext_out[:, :RIM, :] = jnp.zeros((samples, RIM, width), bf16)

    @pl.when(last)
    def _():
        ext_out[:, RIM + slots :, :] = jnp.zeros((samples, RIM, width), bf16)

    def move(sample, carry):
        ext_out[sample, RIM : RIM + slots, :] = rows_ref[sample]
        return carry

    lax.fori_loop(0, samples, move, 0)
    for ref, out in ((held, wide_out), (down_ref, down_out), (tiny_ref, tiny_out)):
        rows = ref.shape[0]
        out[pl.ds(pl.multiple_of(z * rows, 16), rows), :] = ref[...]
    passed = []
    for hop in range(samp - 1):
        origin = lax.rem(z + samp - 1 - hop, samp)
        for kind, out in ((0, wide_out), (1, down_out)):
            copies[hop][kind].wait_recv()
            cell = half(out, origin, core)
            copy = remote(cell, cell, send.at[3 + kind, hop], recv.at[3 + kind, hop], (z, sib))
            copy.start()
            passed.append(copy)
    for hop in range(samp - 1):
        copies[hop][2].wait_recv()
        for copy in copies[hop]:
            copy.wait_send()
    for copy in passed:
        copy.wait()

    @pl.when(~last)
    def _():
        to_right.wait_send()
        to_left.wait_recv()

    @pl.when(~first)
    def _():
        to_left.wait_send()
        to_right.wait_recv()


def edges(weights, tiny_own, rows):
    samp, seq = lax.axis_size("samp"), lax.axis_size("seq")
    samples, slots, width = rows.shape
    place = pl.BlockSpec(memory_space=pltpu.VMEM)
    lanes = sum(part.shape[1] for part in weights[:4])
    return pl.pallas_call(
        functools.partial(edge_kernel, samp, seq),
        out_shape=[
            jax.ShapeDtypeStruct((samp * weights[0].shape[0], lanes), bf16),
            jax.ShapeDtypeStruct((samp * weights[4].shape[0], weights[4].shape[1]), bf16),
            jax.ShapeDtypeStruct((samp * tiny_own.shape[0], tiny_own.shape[1]), bf16),
            jax.ShapeDtypeStruct((samples, slots + 2 * RIM, width), bf16),
        ],
        in_specs=[place] * 7,
        out_specs=[place] * 4,
        scratch_shapes=[
            pltpu.VMEM((weights[0].shape[0], lanes), bf16),
            pltpu.SemaphoreType.DMA((6, samp)),
            pltpu.SemaphoreType.DMA((6, samp)),
        ],
        compiler_params=pltpu.CompilerParams(
            vmem_limit_bytes=vmem_bytes, collective_id=0, has_side_effects=True
        ),
        name="edges",
    )(*weights, tiny_own, rows)


UNIT = 336


def add_into(target, source, lanes=slice(None), rows=48):
    def one(step, carry):
        part = pl.ds(pl.multiple_of(step * rows, 16), rows)
        target[part, lanes] = target[part, lanes] + source[part, :]
        return carry

    lax.fori_loop(0, target.shape[0] // rows, one, 0)


class GradSum:
    head, tail, full = slice(0, 384), slice(384, 768), slice(0, 768)

    def __init__(self, shapes):
        self.shapes = list(shapes)

    def scratch(self):
        half = (UNIT, 384)
        dma = pltpu.SemaphoreType.DMA
        return [
            pltpu.VMEM((4, 4, UNIT, 768), bf16),
            pltpu.VMEM((4, 4, UNIT, 768), bf16),
            pltpu.VMEM((4, 2) + half, bf16),
            pltpu.VMEM((4, 2) + half, bf16),
            pltpu.VMEM((4,) + half, bf16),
            pltpu.VMEM((4,) + half, bf16),
            pltpu.VMEM((3, UNIT, 768), bf16),
            pltpu.VMEM((UNIT, 768), bf16),
            dma((4, 4)),
            dma((4, 4)),
            dma((4, 4)),
            dma((4, 4)),
            dma((4, 4)),
            dma((4, 2)),
            dma((4, 2)),
            dma((3,)),
            dma((3,)),
            dma((3,)),
            dma((3,)),
            dma,
        ]

    def params(self):
        return pltpu.CompilerParams(
            vmem_limit_bytes=vmem_bytes, collective_id=2, has_side_effects=True
        )

    def bind(
        self, grads, shares, mine, theirs, from_x, from_y, last_x, last_y, planes, own_share, *sems
    ):
        self.grads, self.shares, self.own_share = grads, shares, own_share
        self.mine, self.theirs, self.from_x, self.from_y = mine, theirs, from_x, from_y
        self.last_x, self.last_y, self.planes = last_x, last_y, planes
        (
            self.s_sib,
            self.r_sib,
            self.s_own,
            self.s_one,
            self.r_one,
            self.s_two,
            self.r_two,
            self.s_z,
            self.r_z,
            self.s_share,
            self.r_share,
            self.s_out,
        ) = sems
        self.z, self.me, self.sib, self.xn, self.yn, self.dg = places()
        self.core, self.chip = self.me % 2, self.me // 2
        self.chip_x, self.chip_y, self.chip_d = self.xn // 2, self.yn // 2, self.dg // 2
        order = [[p ^ hop for hop in (2, 3, 1, 0)] for p in range(4)]
        self.plane = [pick(self.z, [order[p][r] for p in range(4)]) for r in range(4)]

    def there(self, r, j):
        return remote(
            self.grads.at[2 * j + 1 - self.core, self.plane[r]],
            self.theirs.at[r, j],
            self.s_sib.at[r, j],
            self.r_sib.at[r, j],
            (self.z, self.sib),
        )

    def here(self, r, j):
        return pltpu.make_async_copy(
            self.grads.at[2 * j + self.core, self.plane[r]], self.mine.at[r, j], self.s_own.at[r, j]
        )

    def one(self, r, k):
        chip = (self.chip_x, self.chip_d, self.chip_y, self.chip_d)[k]
        lanes = self.head if k < 2 else self.tail
        target = (self.from_x if k < 2 else self.from_y).at[r, k % 2]
        device = (self.z, self.xn if k < 2 else self.yn)
        return remote(
            self.mine.at[r, chip, :, lanes], target, self.s_one.at[r, k], self.r_one.at[r, k], device
        )

    def two(self, r, k):
        chip, lanes, target, device = (
            (self.chip_y, self.head, self.last_y, self.yn),
            (self.chip_x, self.tail, self.last_x, self.xn),
        )[k]
        return remote(
            self.mine.at[r, chip, :, lanes],
            target.at[r],
            self.s_two.at[r, k],
            self.r_two.at[r, k],
            (self.z, device),
        )

    def across(self, r):
        return remote(
            self.mine.at[r, self.chip],
            self.planes.at[r],
            self.s_z.at[r],
            self.r_z.at[r],
            (self.plane[r], self.me),
        )

    def keep(self):
        return pltpu.make_async_copy(self.own_share, self.shares.at[self.me], self.s_out)

    def share(self, kind):
        device = (self.xn, self.yn, self.sib)[kind]
        return remote(
            self.own_share,
            self.shares.at[self.me],
            self.s_share.at[kind],
            self.r_share.at[kind],
            (self.z, device),
        )

    def shared(self, kind):
        part = self.shares.at[(self.xn, self.yn, self.sib)[kind]]
        return remote(part, part, self.s_share.at[kind], self.r_share.at[kind], (self.z, self.sib))

    def begin(self, r):
        for j in range(4):
            self.there(r, j).start()
            self.here(r, j).start()

    def pairs(self, r):
        for j in range(4):
            self.there(r, j).wait_recv()
            self.here(r, j).wait()
        for j in range(4):
            add_into(self.mine.at[r, j], self.theirs.at[r, j])
        for k in range(4):
            self.one(r, k).start()

    def middle(self, r):
        self.one(r, 1).wait_recv()
        add_into(self.mine.at[r, self.chip_y], self.from_x.at[r, 1], self.head)
        self.two(r, 0).start()
        self.one(r, 3).wait_recv()
        add_into(self.mine.at[r, self.chip_x], self.from_y.at[r, 1], self.tail)
        self.two(r, 1).start()
        self.one(r, 0).wait_recv()
        add_into(self.mine.at[r, self.chip], self.from_x.at[r, 0], self.head)
        self.one(r, 2).wait_recv()
        add_into(self.mine.at[r, self.chip], self.from_y.at[r, 0], self.tail)

    def finish(self, r):
        self.two(r, 0).wait_recv()
        add_into(self.mine.at[r, self.chip], self.last_y.at[r], self.head)
        self.two(r, 1).wait_recv()
        add_into(self.mine.at[r, self.chip], self.last_x.at[r], self.tail)
        if r < 3:
            self.across(r).start()

    def total(self):
        for r in range(3):
            self.across(r).wait_recv()

        def one(step, carry):
            rows = pl.ds(pl.multiple_of(step * 48, 16), 48)
            both = self.mine[3, self.chip, rows, :].astype(f32)
            for r in range(3):
                both += self.planes[r, rows, :].astype(f32)
            self.own_share[rows, :] = both.astype(bf16)
            return carry

        lax.fori_loop(0, UNIT // 48, one, 0)
        for kind in range(3):
            self.share(kind).start()
        self.keep().start()

    def collect(self):
        self.keep().wait()
        for kind in range(3):
            self.shared(kind).wait_recv()
        for kind in range(3):
            self.share(kind).wait_send()
        for r in range(4):
            for j in range(4):
                self.there(r, j).wait_send()
                self.one(r, j).wait_send()
            for k in range(2):
                self.two(r, k).wait_send()
            if r < 3:
                self.across(r).wait_send()

    def hello(self):
        greet(
            [(self.z, self.sib), (self.z, self.xn), (self.z, self.yn)]
            + [(self.plane[r], self.me) for r in range(3)]
            + [(self.z, lax.rem(self.me + 1, 8)), (self.z, lax.rem(self.me + 7, 8))]
        )
        self.begin(0)
        self.begin(1)

    def slot(self, index):
        plan = {
            0: [self.hello],
            1: [lambda: self.pairs(0), lambda: self.begin(2)],
            3: [lambda: self.pairs(1), lambda: self.begin(3)],
            4: [lambda: self.middle(0)],
            6: [lambda: self.pairs(2), lambda: self.finish(0)],
            7: [lambda: self.middle(1)],
            9: [lambda: self.pairs(3), lambda: self.finish(1)],
            10: [lambda: self.middle(2)],
            12: [lambda: self.finish(2)],
            13: [lambda: self.middle(3)],
            14: [lambda: self.finish(3)],
            16: [self.total],
        }
        for at, actions in plan.items():

            @pl.when(index == at)
            def _():
                for action in actions:
                    action()


def small_sum_kernel(
    main,
    tiny,
    own,
    out_ref,
    shares,
    grads,
    cores,
    chips,
    planes,
    share,
    total,
    s_one,
    r_one,
    s_two,
    r_two,
    s_z,
    r_z,
    s_all,
    r_all,
    s_share,
    r_share,
    s_own,
):
    z, me, sib, xn, yn, dg = places()
    core, chip = me % 2, me // 2
    near = (xn, yn, dg)
    parts, samp, rows = grads.shape[:3]
    for part in range(parts):
        for p in range(samp):
            grads[part, p] = main[p, part * rows : (part + 1) * rows, :]
    low, width = 2 * tiny.shape[1], tiny.shape[2]
    for part in range(tiny.shape[1] // rows):
        for p in range(samp):
            grads[low // rows + part, p, :, -width:] = tiny[p, part * rows : (part + 1) * rows, :]
    others = [lax.rem(z + hop, 4) for hop in (1, 2, 3)]
    greet(
        [(z, sib)]
        + [(z, part) for part in near]
        + [(z, part + 1 - 2 * core) for part in near]
        + [(other, me) for other in others]
    )

    def one(j):
        return remote(
            grads.at[2 * j + 1 - core], cores.at[j], s_one.at[j], r_one.at[j], (z, sib)
        )

    width = own.shape[2]
    head, tail, full = slice(0, width // 2), slice(width // 2, width), slice(0, width)

    def give(part, lanes, kind, device):
        target = shares.at[part, :, lanes]
        source = target if kind == 4 else own.at[part, :, lanes]
        return remote(source, target, s_share.at[kind], r_share.at[kind], (z, device))

    kept = [
        pltpu.make_async_copy(own.at[part], shares.at[part], s_own.at[k])
        for k, part in enumerate((me, xn, yn, sib))
    ]
    gifts = [
        give(xn, head, 0, yn),
        give(yn, tail, 1, xn),
        give(xn, full, 2, sib),
        give(yn, full, 3, sib),
    ]
    for copy in kept:
        copy.start()
    for j in range(4):
        one(j).start()
    for j in range(4):
        one(j).wait()
        both = cores[j].astype(f32) + grads[2 * j + core].astype(f32)
        cores[j] = both.astype(bf16)

    def two(k):
        return remote(cores.at[near[k] // 2], chips.at[k], s_two.at[k], r_two.at[k], (z, near[k]))

    for k in range(3):
        two(k).start()
    for gift in gifts:
        gift.start()
    both = cores[chip].astype(f32)
    for k in range(3):
        two(k).wait()
        both += chips[k].astype(f32)
    share[...] = both.astype(bf16)

    def three(k):
        return remote(share.at[others[k]], planes.at[k], s_z.at[k], r_z.at[k], (others[k], me))

    for k in range(3):
        three(k).start()
    give(dg, head, 0, yn).wait_recv()
    give(dg, tail, 1, xn).wait_recv()
    gifts.append(give(dg, full, 4, sib))
    gifts[-1].start()
    both = share[z].astype(f32)
    for k in range(3):
        three(k).wait()
        both += planes[k].astype(f32)
    total[me] = both.astype(bf16)

    receivers = [sib] + list(near) + [part + 1 - 2 * core for part in near]

    def four(k, part, device):
        return remote(total.at[part], total.at[part], s_all.at[k], r_all.at[k], (z, device))

    for k, device in enumerate(receivers):
        four(k, me, device).start()
    for k, device in enumerate(receivers):
        four(k, device, device).wait_recv()
    for k, device in enumerate(receivers):
        four(k, me, device).wait_send()
    for part in range(parts):
        out_ref[part * rows : (part + 1) * rows, :] = total[part]
    for kind in (2, 3, 4):
        give(sib, full, kind, sib).wait_recv()
    for copy in kept:
        copy.wait()
    for gift in gifts:
        gift.wait_send()


def small_sums(main, tiny, own):
    seq = lax.axis_size("seq")
    samp, rows, width = main.shape
    rows //= seq
    dma = pltpu.SemaphoreType.DMA
    return pl.pallas_call(
        small_sum_kernel,
        out_shape=[
            jax.ShapeDtypeStruct((seq * rows, width), bf16),
            jax.ShapeDtypeStruct(own.shape, bf16),
        ],
        in_specs=[pl.BlockSpec(memory_space=pltpu.VMEM)] * 3,
        out_specs=[
            pl.BlockSpec(memory_space=pltpu.VMEM),
            pl.BlockSpec(memory_space=pl.ANY),
        ],
        scratch_shapes=[
            pltpu.VMEM((seq, samp, rows, width), bf16),
            pltpu.VMEM((4, samp, rows, width), bf16),
            pltpu.VMEM((3, samp, rows, width), bf16),
            pltpu.VMEM((3, rows, width), bf16),
            pltpu.VMEM((samp, rows, width), bf16),
            pltpu.VMEM((seq, rows, width), bf16),
            dma((4,)),
            dma((4,)),
            dma((3,)),
            dma((3,)),
            dma((3,)),
            dma((3,)),
            dma((7,)),
            dma((7,)),
            dma((5,)),
            dma((5,)),
            dma((4,)),
        ],
        compiler_params=pltpu.CompilerParams(
            vmem_limit_bytes=vmem_bytes, collective_id=3, has_side_effects=True
        ),
        name="small_sums",
    )(main, tiny, own)


def pair_stats(pairs, fold):
    upper, lower = square_sums(fold, pairs.astype(f32) * pairs.astype(f32))
    features = pairs.shape[0] // WIN_Q
    mean = mm(fold, pairs) * (1.0 / features)
    square = (mm(fold, upper) + mm(fold, lower)) * (1.0 / features)
    var = jnp.maximum(square - mean * mean, 0.0)
    inv_std = lax.rsqrt(var + norm_eps)
    return mean, inv_std


def pair_fold(features):
    shape = (WIN_Q, WIN_Q * features)
    row = lax.broadcasted_iota(jnp.int32, shape, 0)
    column = lax.broadcasted_iota(jnp.int32, shape, 1)
    return jnp.where(column // features == row, 1.0, 0.0).astype(bf16)


def atom_fwd_kernel(
    gather,
    starts,
    ext_ref,
    pairs_ref,
    spread_ref,
    blocked_ref,
    share_ref,
    wide_ref,
    down_ref,
    qbias_ref,
    *refs,
):
    count = len(gather.shapes) if gather is not None else 0
    shards, refs = refs[:count], refs[count:]
    (
        pooled_ref,
        query_ref,
        keyval_ref,
        gate_ref,
        probs_ref,
        attend_ref,
        mid_ref,
    ), refs = refs[:7], refs[7:]
    fulls, refs = refs[:count], refs[count:]
    bias_s, sems = refs[0], refs[1:]
    width = ext_ref.shape[-1]
    head_dim = width // ATOM_HEADS
    scale = float(head_dim) ** (-0.5)
    slots = query_ref.shape[1]
    windows = slots // WIN_Q
    hidden_width = down_ref.shape[0]
    model_width = pooled_ref.shape[-1]
    features = pairs_ref.shape[1] // WIN_Q
    sample = pl.program_id(0)
    if gather is not None:
        gather.step(sample, shards, fulls, *sems)

    @pl.when(sample == 0)
    def _():
        fold = pair_fold(features)
        spread = spread_ref[...]
        spread_sum = jnp.sum(spread.astype(f32), -1, keepdims=True)
        first_lane = jnp.where(
            lax.broadcasted_iota(jnp.int32, (ATOM_HEADS * WIN_Q, LANES), 1) == 0, 1.0, 0.0
        ).astype(bf16)

        fill = jnp.full((ATOM_HEADS * WIN_Q, WIN_K), masked_score, f32)

        def one(duo, carry):
            base = pl.multiple_of(duo * 2 * WIN_Q, 2 * WIN_Q)
            blocked = mm_nt(first_lane, blocked_ref[pl.ds(base, 2 * WIN_K), :].astype(bf16))
            for part in range(2):
                win = duo * 2 + part
                pairs = pairs_ref[win]
                mean, inv_std = pair_stats(pairs, fold)
                mean = jnp.concatenate([mean] * ATOM_HEADS, 0)
                inv_std = jnp.concatenate([inv_std] * ATOM_HEADS, 0)
                bias = inv_std * (mm(spread, pairs) - mean * spread_sum)
                bias = pltpu.roll(jnp.concatenate([bias, fill], 1), starts[win] - base, 1) + blocked
                for head in range(ATOM_HEADS):
                    low = (head * 2 + part) * WIN_Q
                    bias_s[duo, low : low + WIN_Q, :] = bias[head * WIN_Q : (head + 1) * WIN_Q]
            return carry

        lax.fori_loop(0, windows // 2, one, 0)

    rows = ext_ref[0].astype(f32)
    normed_low = norm_stats(rows)[0].astype(bf16)
    key_val = mm(normed_low, wide_ref[:, width : 3 * width]).astype(bf16)
    keyval_ref[0] = key_val
    own_low = normed_low[RIM : RIM + slots]
    query_ref[0] = (mm(own_low, wide_ref[:, :width]) + qbias_ref[...]).astype(bf16)
    gate_ref[0] = mm(own_low, wide_ref[:, 3 * width : 4 * width])

    masks = head_masks(2 * WIN_Q, width, ATOM_HEADS, head_dim, 0)

    def two_windows(duo):
        first = pl.multiple_of(duo * 2 * WIN_Q, 2 * WIN_Q)
        span = pl.ds(first, 2 * WIN_K)
        own = pl.ds(first, 2 * WIN_Q)
        stacked = head_stack(query_ref[0, own, :], ATOM_HEADS, head_dim, 0, masks)
        scores = mm_nt(stacked, keyval_ref[0, span, :width]) * scale + bias_s[duo]
        exp_scores = jnp.exp(scores - jnp.max(scores, -1, keepdims=True))
        probs = exp_scores * (1.0 / jnp.sum(exp_scores, -1, keepdims=True))
        probs_low = probs.astype(bf16)
        probs_ref[0, duo] = probs_low
        attend_ref[0, own, :] = head_fold(
            mm(probs_low, keyval_ref[0, span, width:]), ATOM_HEADS, head_dim, 0
        )

    def some_windows(step, carry):
        for part in range(2):
            two_windows(step * 2 + part)
        return carry

    lax.fori_loop(0, windows // 4, some_windows, 0)

    gated_low = (attend_ref[0] * sigmoid(gate_ref[0])).astype(bf16)
    offset = 4 * width
    upw = wide_ref[:, offset : offset + 2 * hidden_width]
    offset += 2 * hidden_width
    pool_weight = wide_ref[:, offset : offset + model_width]
    outw = wide_ref[:, offset + model_width : offset + model_width + width]
    mid = rows[RIM : RIM + slots] + mm(gated_low, outw)
    mid_ref[0] = mid
    ffn_low = norm_stats(mid)[0].astype(bf16)
    upper = mm(ffn_low, upw)
    first_half, second_half = upper[:, :hidden_width], upper[:, hidden_width:]
    hidden = (first_half * sigmoid(first_half) * second_half).astype(bf16)
    final_low = (mid + mm(hidden, down_ref[...])).astype(bf16)
    pool_pre = mm(final_low, pool_weight)
    share = share_ref[...]
    for lane in range(0, model_width, LANES):
        part = pool_pre[:, lane : lane + LANES]
        part = part * sigmoid(part) * share
        pooled_ref[0, :, lane : lane + LANES] = jnp.sum(
            part.reshape(slots // MAX_ATOMS, MAX_ATOMS, LANES), 1
        )
    if gather is not None:
        gather.last(sample, shards, fulls, *sems)


def atom_forward(ext, starts, pairs, spread, blocked, share, wide, down, qbias, gather, shards):
    samples, ext_slots, width = ext.shape
    slots = ext_slots - 2 * RIM
    tokens = slots // MAX_ATOMS
    windows = slots // WIN_Q
    model_width = wide.shape[1] - 5 * width - 2 * down.shape[0]
    stack = ATOM_HEADS * WIN_Q
    outs = (
        ((tokens, model_width), f32),
        ((slots, width), bf16),
        ((ext_slots, 2 * width), bf16),
        ((slots, width), f32),
        ((windows // 2, 2 * stack, 2 * WIN_K), bf16),
        ((slots, width), f32),
        ((slots, width), f32),
    )
    place = pl.BlockSpec(memory_space=pl.ANY)
    results = pl.pallas_call(
        functools.partial(atom_fwd_kernel, gather),
        out_shape=[jax.ShapeDtypeStruct((samples,) + shape, kind) for shape, kind in outs]
        + [jax.ShapeDtypeStruct(shape, bf16) for shape in (gather.full_shapes() if gather else [])],
        grid=(samples,),
        in_specs=[
            pl.BlockSpec(memory_space=pltpu.SMEM),
            per_sample((ext_slots, width)),
            whole(pairs.shape),
            whole(spread.shape),
            whole(blocked.shape),
            whole(share.shape),
            whole(wide.shape),
            whole(down.shape),
            whole(qbias.shape),
        ]
        + [place] * len(shards),
        out_specs=[per_sample(shape) for shape, _ in outs] + [place] * len(shards),
        scratch_shapes=[pltpu.VMEM((windows // 2, 2 * stack, 2 * WIN_K), f32)]
        + (gather.scratch() if gather else []),
        compiler_params=gather.params() if gather else params(),
        name="atom_forward",
    )(starts, ext, pairs, spread, blocked, share, wide, down, qbias, *shards)
    return results[0], results[1:7], results[7:]


def atom_bwd_dense(sample_refs, consts, accs, attlow_s, gate_grad_at, mid_grad_at):
    grad_ref, query_ref, gate_ref, attend_ref, mid_ref = sample_refs
    share_ref, wide_ref, down_ref = consts
    outw_ref, upw_ref, downw_ref, pool_ref = accs
    width = query_ref.shape[-1]
    slots = query_ref.shape[1]
    hidden_width = down_ref.shape[0]
    model_width = grad_ref.shape[-1]
    tokens = grad_ref.shape[1]
    offset = 4 * width
    upw = wide_ref[:, offset : offset + 2 * hidden_width]
    offset += 2 * hidden_width
    pool_weight = wide_ref[:, offset : offset + model_width]
    outw = wide_ref[:, offset + model_width : offset + model_width + width]
    down = down_ref[...]

    mid = mid_ref[0]
    normed_mid, inv_mid = norm_stats(mid)
    ffn_low = normed_mid.astype(bf16)
    upper = mm(ffn_low, upw)
    first_half, second_half = upper[:, :hidden_width], upper[:, hidden_width:]
    sig_first = sigmoid(first_half)
    hidden = (first_half * sig_first * second_half).astype(bf16)
    final_low = (mid + mm(hidden, down)).astype(bf16)
    pool_pre = mm(final_low, pool_weight)
    share = share_ref[...]
    pool_parts = []
    for lane in range(0, model_width, LANES):
        part = pool_pre[:, lane : lane + LANES]
        grad = jnp.broadcast_to(
            grad_ref[0, :, lane : lane + LANES][:, None, :], (tokens, MAX_ATOMS, LANES)
        ).reshape(slots, LANES)
        sig_pool = sigmoid(part)
        pool_parts.append((grad * share * sig_pool * (1.0 + part * (1.0 - sig_pool))).astype(bf16))
    pool_grad = jnp.concatenate(pool_parts, 1)
    final_grad = mm_nt(pool_grad, pool_weight)
    pool_ref[...] += mm_tn(final_low, pool_grad)
    branch_low = final_grad.astype(bf16)
    hidden_grad = mm_nt(branch_low, down)
    first_grad = hidden_grad * second_half * sig_first * (1.0 + first_half * (1.0 - sig_first))
    second_grad = hidden_grad * first_half * sig_first
    upper_grad = jnp.concatenate([first_grad.astype(bf16), second_grad.astype(bf16)], 1)
    downw_ref[...] += mm_tn(hidden, branch_low)
    upw_ref[...] += mm_tn(ffn_low, upper_grad)
    mid_grad = final_grad + norm_back(normed_mid, inv_mid, mm_nt(upper_grad, upw))
    mid_grad_at[...] = mid_grad
    out_low = mid_grad.astype(bf16)
    gated_grad = mm_nt(out_low, outw)
    sig_gate = sigmoid(gate_ref[0])
    attend = attend_ref[0]
    gated_low = (attend * sig_gate).astype(bf16)
    outw_ref[...] += mm_tn(gated_low, out_low)
    attlow_s[...] = (gated_grad * sig_gate).astype(bf16)
    gate_grad_at[...] = (gated_grad * attend * sig_gate * (1.0 - sig_gate)).astype(bf16)


def atom_bwd_windows(sample_refs, scratch):
    query_ref, keyval_ref, probs_ref = sample_refs
    acck_s, accv_s, bias_s, attlow_s, dq_s = scratch
    width = query_ref.shape[-1]
    head_dim = width // ATOM_HEADS
    scale = float(head_dim) ** (-0.5)
    windows = query_ref.shape[1] // WIN_Q
    acck_s[...] = jnp.zeros_like(acck_s)
    accv_s[...] = jnp.zeros_like(accv_s)
    masks = head_masks(2 * WIN_Q, width, ATOM_HEADS, head_dim, 0)

    def two_windows(duo):
        first = pl.multiple_of(duo * 2 * WIN_Q, 2 * WIN_Q)
        span = pl.ds(first, 2 * WIN_K)
        own = pl.ds(first, 2 * WIN_Q)
        queries = head_stack(query_ref[0, own, :], ATOM_HEADS, head_dim, 0, masks)
        att = head_stack(attlow_s[own, :], ATOM_HEADS, head_dim, 0, masks)
        probs_low = probs_ref[0, duo]
        probs = probs_low.astype(f32)
        prob_grad = mm_nt(att, keyval_ref[0, span, width:])
        delta = jnp.sum(prob_grad * probs, -1, keepdims=True)
        score_low = (probs * (prob_grad - delta)).astype(bf16)
        bias_s[duo] += score_low.astype(f32)
        dq_s[own, :] = (
            head_fold(mm(score_low, keyval_ref[0, span, :width]), ATOM_HEADS, head_dim, 0) * scale
        )
        acck_s[span, :] += mm_tn(score_low, queries) * scale
        accv_s[span, :] += mm_tn(probs_low, att)

    def some_windows(step, carry):
        for part in range(2):
            two_windows(step * 2 + part)
        return carry

    lax.fori_loop(0, windows // 4, some_windows, 0)


def atom_bwd_pairs(starts, pairs_ref, bias_s, pairw_ref, pairm_ref):
    fold = pair_fold(pairs_ref.shape[1] // WIN_Q)

    def one(duo, carry):
        for part in range(2):
            win = duo * 2 + part
            pairs = pairs_ref[win]
            mean, inv_std = pair_stats(pairs, fold)
            lows = [(head * 2 + part) * WIN_Q for head in range(ATOM_HEADS)]
            placed = jnp.concatenate([bias_s[duo, low : low + WIN_Q, :] for low in lows], 0)
            shift = starts[win] - duo * 2 * WIN_Q
            grad = pltpu.roll(placed, lax.rem(2 * WIN_K - shift, 2 * WIN_K), 1)[:, :WIN_K]
            scaled = grad * jnp.concatenate([inv_std] * ATOM_HEADS, 0)
            pairm_ref[...] += scaled * jnp.concatenate([mean] * ATOM_HEADS, 0)
            upper = scaled.astype(bf16)
            lower = (scaled - upper.astype(f32)).astype(bf16)
            pairw_ref[...] += mm_nt(upper, pairs) + mm_nt(lower, pairs)
        return carry

    lax.fori_loop(0, pairs_ref.shape[0] // 2, one, 0)


def atom_bwd_kernel(
    starts,
    grad_ref,
    query_ref,
    keyval_ref,
    gate_ref,
    probs_ref,
    attend_ref,
    mid_ref,
    pairs_ref,
    share_ref,
    wide_ref,
    down_ref,
    mix_ref,
    own_ref,
    left_ref,
    right_ref,
    midgrad_ref,
    qbias_ref,
    outw_ref,
    upw_ref,
    downw_ref,
    pool_ref,
    pairw_ref,
    pairm_ref,
    *scratch,
):
    acck_s, accv_s, bias_s, attlow_s, dq_s = scratch
    width = query_ref.shape[-1]
    slots = query_ref.shape[1]
    sample = pl.program_id(0)

    @pl.when(sample == 0)
    def _():
        for ref in (qbias_ref, outw_ref, upw_ref, downw_ref, pool_ref, pairw_ref, pairm_ref, bias_s):
            ref[...] = jnp.zeros_like(ref)

    atom_bwd_dense(
        (grad_ref, query_ref, gate_ref, attend_ref, mid_ref),
        (share_ref, wide_ref, down_ref),
        (outw_ref, upw_ref, downw_ref, pool_ref),
        attlow_s,
        mix_ref.at[0, :, width:],
        midgrad_ref.at[0],
    )
    atom_bwd_windows((query_ref, keyval_ref, probs_ref), scratch)
    query_grad = dq_s[...]
    qbias_ref[...] += jnp.sum(query_grad, 0, keepdims=True)
    mix_ref[0, :, :width] = query_grad.astype(bf16)
    for ref, low, high in (
        (own_ref, RIM, RIM + slots),
        (left_ref, 0, RIM),
        (right_ref, RIM + slots, slots + 2 * RIM),
    ):
        ref[0, :, :width] = acck_s[low:high, :].astype(ref.dtype)
        ref[0, :, width:] = accv_s[low:high, :].astype(ref.dtype)

    @pl.when(sample == pl.num_programs(0) - 1)
    def _():
        atom_bwd_pairs(starts, pairs_ref, bias_s, pairw_ref, pairm_ref)


def atom_bwd_sum_kernel(
    summing,
    starts,
    grad_ref,
    query_ref,
    keyval_ref,
    gate_ref,
    probs_ref,
    attend_ref,
    mid_ref,
    rows_ref,
    pairs_ref,
    share_ref,
    wide_ref,
    down_ref,
    units_ref,
    atomgrad_ref,
    qbias_ref,
    pairw_ref,
    pairm_ref,
    small_ref,
    shares_ref,
    acck_s,
    accv_s,
    bias_s,
    attlow_s,
    dq_s,
    mix_s,
    midgrad_s,
    outw_s,
    upw_s,
    downw_s,
    pool_s,
    proj_s,
    own_s,
    to_left,
    to_right,
    from_left,
    from_right,
    s_rim,
    r_rim,
    *sums,
):
    summing.bind(units_ref, shares_ref, *sums)
    z, me = lax.axis_index("samp"), lax.axis_index("seq")
    seq = lax.axis_size("seq")
    first_place, last_place = me == 0, me == seq - 1
    width = query_ref.shape[-1]
    slots = query_ref.shape[1]
    step = pl.program_id(0)
    samples = pl.num_programs(0) - 1
    summing.slot(2 * step)

    def rim(b, side):
        ends = ((to_left, from_right, me - 1), (to_right, from_left, me + 1))[side]
        source, target, device = ends
        return remote(source.at[b], target.at[b], s_rim.at[side, b], r_rim.at[side, b], (z, device))

    def arrived(b, side):
        target = (from_right, from_left)[side]
        return remote(
            target.at[b], target.at[b], s_rim.at[side, b], r_rim.at[side, b], (z, lax.rem(me + 1, seq))
        )

    @pl.when(step == 0)
    def _():
        for ref in (qbias_ref, outw_s, upw_s, downw_s, pool_s, proj_s, pairw_ref, pairm_ref, bias_s):
            ref[...] = jnp.zeros_like(ref)

        @pl.when(first_place)
        def _():
            from_left[...] = jnp.zeros_like(from_left)

        @pl.when(last_place)
        def _():
            from_right[...] = jnp.zeros_like(from_right)

    slot_now = step % 2

    @pl.when(step < samples)
    def _():
        atom_bwd_dense(
            (grad_ref, query_ref, gate_ref, attend_ref, mid_ref),
            (share_ref, wide_ref, down_ref),
            (outw_s, upw_s, downw_s, pool_s),
            attlow_s,
            mix_s.at[slot_now, :, width:],
            midgrad_s.at[slot_now],
        )

    summing.slot(2 * step + 1)

    @pl.when(step < samples)
    def _():
        atom_bwd_windows(
            (query_ref, keyval_ref, probs_ref), (acck_s, accv_s, bias_s, attlow_s, dq_s)
        )
        query_grad = dq_s[...]
        qbias_ref[...] += jnp.sum(query_grad, 0, keepdims=True)
        mix_s[slot_now, :, :width] = query_grad.astype(bf16)
        for ref, low in ((to_left, 0), (to_right, RIM + slots)):
            ref[step, :, :width] = acck_s[low : low + RIM, :].astype(bf16)
            ref[step, :, width:] = accv_s[low : low + RIM, :].astype(bf16)

        @pl.when(~first_place)
        def _():
            rim(step, 0).start()

        @pl.when(~last_place)
        def _():
            rim(step, 1).start()

    @pl.when(step > 0)
    def _():
        b = step - 1

        @pl.when(~first_place)
        def _():
            arrived(b, 1).wait_recv()

        @pl.when(~last_place)
        def _():
            arrived(b, 0).wait_recv()

        normed, inv_std = norm_stats(rows_ref[0].astype(f32))
        parts = []
        for lanes in (slice(0, width), slice(width, 2 * width)):
            own = own_s[:, lanes]
            begin = own[:RIM] + from_left[b, :, lanes].astype(f32)
            end = own[slots - RIM :] + from_right[b, :, lanes].astype(f32)
            parts.append(jnp.concatenate([begin, own[RIM : slots - RIM], end], 0).astype(bf16))
        before = mix_s.at[1 - slot_now]
        mix = jnp.concatenate([before[:, :width], parts[0], parts[1], before[:, width:]], 1)
        proj_s[...] += mm_tn(normed.astype(bf16), mix)
        normed_grad = mm_nt(mix, wide_ref[:, : 4 * width])
        atomgrad_ref[0] = midgrad_s[1 - slot_now] + norm_back(normed, inv_std, normed_grad)

    @pl.when(step < samples)
    def _():
        own_s[:, :width] = acck_s[RIM : RIM + slots, :]
        own_s[:, width:] = accv_s[RIM : RIM + slots, :]

    @pl.when(step == samples)
    def _():
        atom_bwd_pairs(starts, pairs_ref, bias_s, pairw_ref, pairm_ref)
        samp = small_ref.shape[0]
        rows = width // samp
        for p in range(samp):
            span = slice(p * rows, (p + 1) * rows)
            small_ref[p, :rows, :] = pool_s[span, :].astype(bf16)
            small_ref[p, rows : 2 * rows, : 4 * width] = proj_s[span, :].astype(bf16)
            for part in range(2):
                low = (2 * p + part) * rows
                small_ref[p, rows : 2 * rows, (4 + part) * width : (5 + part) * width] = downw_s[
                    low : low + rows, :
                ].astype(bf16)
            small_ref[p, 2 * rows : 3 * rows, : 4 * width] = upw_s[span, :].astype(bf16)
            small_ref[p, 2 * rows : 3 * rows, 4 * width : 5 * width] = outw_s[span, :].astype(bf16)
            small_ref[p, 2 * rows : 3 * rows, 5 * width :] = jnp.zeros((rows, width), bf16)
            small_ref[p, 3 * rows :, :] = jnp.zeros((rows, 6 * width), bf16)
        summing.collect()

        def sent(b, carry):
            @pl.when(~first_place)
            def _():
                rim(b, 0).wait_send()

            @pl.when(~last_place)
            def _():
                rim(b, 1).wait_send()

            return carry

        lax.fori_loop(0, samples, sent, 0)


def atom_backward_sum(grad, starts, stored, rows, pairs, share, wide, down, summing, units):
    query = stored[0]
    samples, slots, width = query.shape
    samp = lax.axis_size("samp")
    ext_slots = slots + 2 * RIM
    windows = slots // WIN_Q
    model_width = grad.shape[-1]
    hidden_width = down.shape[0]
    stack = ATOM_HEADS * WIN_Q
    place = pl.BlockSpec(memory_space=pl.ANY)

    def now(shape):
        return pl.BlockSpec(
            (1,) + shape, lambda g: (jnp.minimum(g, samples - 1),) + (0,) * len(shape)
        )

    def late(shape):
        return pl.BlockSpec((1,) + shape, lambda g: (jnp.maximum(g - 1, 0),) + (0,) * len(shape))

    dma = pltpu.SemaphoreType.DMA
    rim_shape = (samples, RIM, 2 * width)
    small_shape = (samp, 4 * width // samp, model_width)
    return pl.pallas_call(
        functools.partial(atom_bwd_sum_kernel, summing),
        out_shape=[
            jax.ShapeDtypeStruct(rows.shape, f32),
            jax.ShapeDtypeStruct((1, width), f32),
            jax.ShapeDtypeStruct((stack, pairs.shape[1]), f32),
            jax.ShapeDtypeStruct((stack, WIN_K), f32),
            jax.ShapeDtypeStruct(small_shape, bf16),
            jax.ShapeDtypeStruct((8, UNIT, 768), bf16),
        ],
        grid=(samples + 1,),
        in_specs=[pl.BlockSpec(memory_space=pltpu.SMEM), now(grad.shape[1:])]
        + [now(part.shape[1:]) for part in stored]
        + [late(rows.shape[1:])]
        + [whole(part.shape) for part in (pairs, share, wide, down)]
        + [place],
        out_specs=[
            late(rows.shape[1:]),
            whole((1, width)),
            whole((stack, pairs.shape[1])),
            whole((stack, WIN_K)),
            whole(small_shape),
            place,
        ],
        scratch_shapes=[
            pltpu.VMEM((ext_slots, width), f32),
            pltpu.VMEM((ext_slots, width), f32),
            pltpu.VMEM((windows // 2, 2 * stack, 2 * WIN_K), f32),
            pltpu.VMEM((slots, width), bf16),
            pltpu.VMEM((slots, width), f32),
            pltpu.VMEM((2, slots, 2 * width), bf16),
            pltpu.VMEM((2, slots, width), f32),
            pltpu.VMEM((width, width), f32),
            pltpu.VMEM((width, 2 * hidden_width), f32),
            pltpu.VMEM((hidden_width, width), f32),
            pltpu.VMEM((width, model_width), f32),
            pltpu.VMEM((width, 4 * width), f32),
            pltpu.VMEM((slots, 2 * width), f32),
            pltpu.VMEM(rim_shape, bf16),
            pltpu.VMEM(rim_shape, bf16),
            pltpu.VMEM(rim_shape, bf16),
            pltpu.VMEM(rim_shape, bf16),
            dma((2, samples)),
            dma((2, samples)),
        ]
        + summing.scratch(),
        compiler_params=summing.params(),
        name="atom_backward",
    )(starts, grad, *stored, rows, pairs, share, wide, down, units)


def unpack_kernel(units_ref, small_ref, proj_ref, up_ref, down_ref, cond_ref, outw_ref, *atoms):
    proj_ref[...] = units_ref[0, :192, :384].astype(f32)
    up_ref[...] = units_ref[0, :192, 384:].astype(f32)
    down_ref[...] = units_ref[0, 192:240, :].astype(f32)
    cond_ref[:, :768] = units_ref[0, 240:288, :].astype(f32)
    cond_ref[:, 768:] = units_ref[0, 288:336, :384].astype(f32)
    outw_ref[...] = units_ref[0, 288:336, 384:].astype(f32)

    @pl.when(pl.program_id(0) == 0)
    def _():
        pool_ref, atomproj_ref, atomdown_ref, atomup_ref, atomout_ref, tiny_ref = atoms
        rows, width = atomout_ref.shape
        pool_ref[...] = small_ref[:rows, :].astype(f32)
        atomproj_ref[...] = small_ref[rows : 2 * rows, : 4 * width].astype(f32)
        for part in range(2):
            atomdown_ref[part * rows : (part + 1) * rows, :] = small_ref[
                rows : 2 * rows, (4 + part) * width : (5 + part) * width
            ].astype(f32)
        atomup_ref[...] = small_ref[2 * rows : 3 * rows, : 4 * width].astype(f32)
        atomout_ref[...] = small_ref[2 * rows : 3 * rows, 4 * width : 5 * width].astype(f32)
        tiny_ref[...] = small_ref[2 * rows : 3 * rows, 5 * width :].astype(f32)


def unpack(units, small, shapes, rows, width):
    outs = list(shapes) + [
        (rows, 6 * width),
        (rows, 4 * width),
        (2 * rows, width),
        (rows, 4 * width),
        (rows, width),
        (rows, width),
    ]
    specs = [
        pl.BlockSpec((192, 384), lambda s: (0, s)),
        pl.BlockSpec((192, 384), lambda s: (0, s)),
        pl.BlockSpec((48, 768), lambda s: (s, 0)),
        pl.BlockSpec((48, 1152), lambda s: (s // 4, s % 4)),
        pl.BlockSpec((48, 384), lambda s: (s // 2, s % 2)),
    ]
    return pl.pallas_call(
        unpack_kernel,
        out_shape=[jax.ShapeDtypeStruct(shape, f32) for shape in outs],
        grid=(8,),
        in_specs=[pl.BlockSpec((1, UNIT, 768), lambda s: (s, 0, 0)), whole(small.shape)],
        out_specs=specs + [whole(shape) for shape in outs[5:]],
        compiler_params=params(),
        name="unpack",
    )(units, small)


def atom_backward(grad, starts, stored, pairs, share, wide, down):
    query = stored[0]
    samples, slots, width = query.shape
    ext_slots = slots + 2 * RIM
    windows = slots // WIN_Q
    model_width = grad.shape[-1]
    hidden_width = down.shape[0]
    stack = ATOM_HEADS * WIN_Q
    outs = (
        ((slots, 2 * width), bf16),
        ((slots, 2 * width), f32),
        ((RIM, 2 * width), bf16),
        ((RIM, 2 * width), bf16),
        ((slots, width), f32),
    )
    totals = (
        (1, width),
        (width, width),
        (width, 2 * hidden_width),
        (hidden_width, width),
        (width, model_width),
        (stack, pairs.shape[1]),
        (stack, WIN_K),
    )
    return pl.pallas_call(
        atom_bwd_kernel,
        out_shape=[jax.ShapeDtypeStruct((samples,) + shape, kind) for shape, kind in outs]
        + [jax.ShapeDtypeStruct(shape, f32) for shape in totals],
        grid=(samples,),
        in_specs=[pl.BlockSpec(memory_space=pltpu.SMEM), per_sample(grad.shape[1:])]
        + [per_sample(part.shape[1:]) for part in stored]
        + [whole(part.shape) for part in (pairs, share, wide, down)],
        out_specs=[per_sample(shape) for shape, _ in outs] + [whole(shape) for shape in totals],
        scratch_shapes=[
            pltpu.VMEM((ext_slots, width), f32),
            pltpu.VMEM((ext_slots, width), f32),
            pltpu.VMEM((windows // 2, 2 * stack, 2 * WIN_K), f32),
            pltpu.VMEM((slots, width), bf16),
            pltpu.VMEM((slots, width), f32),
        ],
        compiler_params=params(),
        name="atom_backward",
    )(starts, grad, *stored, pairs, share, wide, down)


def atom_input_kernel(
    rows_ref, mix_ref, own_ref, left_ref, right_ref, midgrad_ref, wide_ref, grad_ref, proj_ref
):
    width = rows_ref.shape[-1]

    @pl.when(pl.program_id(0) == 0)
    def _():
        proj_ref[...] = jnp.zeros_like(proj_ref)

    normed, inv_std = norm_stats(rows_ref[0].astype(f32))
    slots = normed.shape[0]
    own = own_ref[0]
    head = own[:RIM] + left_ref[0].astype(f32)
    tail = own[slots - RIM :] + right_ref[0].astype(f32)
    own = jnp.concatenate([head, own[RIM : slots - RIM], tail], 0).astype(bf16)
    mix = jnp.concatenate([mix_ref[0, :, :width], own, mix_ref[0, :, width:]], 1)
    proj_ref[...] += mm_tn(normed.astype(bf16), mix)
    normed_grad = mm_nt(mix, wide_ref[:, : 4 * width])
    grad_ref[0] = midgrad_ref[0] + norm_back(normed, inv_std, normed_grad)


def atom_input_backward(rows, mix, own, left, right, midgrad, wide):
    samples, slots, width = rows.shape
    return pl.pallas_call(
        atom_input_kernel,
        out_shape=[
            jax.ShapeDtypeStruct(rows.shape, f32),
            jax.ShapeDtypeStruct((width, 4 * width), f32),
        ],
        grid=(samples,),
        in_specs=[per_sample(part.shape[1:]) for part in (rows, mix, own, left, right, midgrad)]
        + [whole(wide.shape)],
        out_specs=[per_sample((slots, width)), whole((width, 4 * width))],
        compiler_params=params(),
        name="atom_input_backward",
    )(rows, mix, own, left, right, midgrad, wide)


def row_stats(pairs, ones_op, weights):
    count = weights.shape[0]
    both = mm_nt(jnp.concatenate([weights, ones_op], 0), pairs)
    upper, lower = square_sums(ones_op, pairs.astype(f32) * pairs.astype(f32))
    features = pairs.shape[1]
    mean = both[count : count + 1] * (1.0 / features)
    square = (mm_nt(ones_op, upper) + mm_nt(ones_op, lower))[:1] * (1.0 / features)
    var = jnp.maximum(square - mean * mean, 0.0)
    return both[:count], mean, lax.rsqrt(var + norm_eps)


def pair_bias_kernel(pair_ref, weight_ref, bias_ref):
    weights = weight_ref[...]
    ones_op = jnp.ones((16, weights.shape[1]), bf16)
    weight_sum = jnp.sum(weights.astype(f32), -1, keepdims=True)
    for row in range(pair_ref.shape[0]):
        product, mean, inv_std = row_stats(pair_ref[row], ones_op, weights)
        bias_ref[:, row, :] = inv_std * (product - mean * weight_sum)


def pair_bias(pairs, weights):
    rows, keys, features = pairs.shape
    heads = weights.shape[0]
    return pl.pallas_call(
        pair_bias_kernel,
        out_shape=jax.ShapeDtypeStruct((heads, rows, keys), f32),
        grid=(rows // 8,),
        in_specs=[pl.BlockSpec((8, keys, features), lambda i: (i, 0, 0)), whole(weights.shape)],
        out_specs=pl.BlockSpec((heads, 8, keys), lambda i: (0, i, 0)),
        compiler_params=params(),
        name="pair_bias",
    )(pairs, weights)


def pair_grad_kernel(pair_ref, grad_ref, weight_ref, total_ref, mean_ref):
    @pl.when(pl.program_id(0) == 0)
    def _():
        total_ref[...] = jnp.zeros_like(total_ref)
        mean_ref[...] = jnp.zeros_like(mean_ref)

    heads = grad_ref.shape[0]
    ones_op = jnp.ones((16, pair_ref.shape[2]), bf16)
    total = jnp.zeros(total_ref.shape, f32)
    means = jnp.zeros(mean_ref.shape, f32)
    for row in range(pair_ref.shape[0]):
        pairs = pair_ref[row]
        _, mean, inv_std = row_stats(pairs, ones_op, weight_ref[...])
        scaled = grad_ref[:, row, :] * inv_std
        means += scaled * mean
        upper = scaled.astype(bf16)
        lower = (scaled - upper.astype(f32)).astype(bf16)
        both = mm(jnp.concatenate([upper, lower], 0), pairs)
        total += both[:heads] + both[heads:]
    total_ref[...] += total
    mean_ref[...] += means


def pair_grad(pairs, grads, weights):
    rows, keys, features = pairs.shape
    heads = grads.shape[0]
    total, means = pl.pallas_call(
        pair_grad_kernel,
        out_shape=[
            jax.ShapeDtypeStruct((heads, features), f32),
            jax.ShapeDtypeStruct((heads, keys), f32),
        ],
        grid=(rows // 8,),
        in_specs=[
            pl.BlockSpec((8, keys, features), lambda i: (i, 0, 0)),
            pl.BlockSpec((heads, 8, keys), lambda i: (0, i, 0)),
            whole(weights.shape),
        ],
        out_specs=[whole((heads, features)), whole((heads, keys))],
        compiler_params=params(),
        name="pair_grad",
    )(pairs, grads, weights)
    return total - jnp.sum(means, -1, keepdims=True)


def head_groups(width, heads):
    head_dim = width // heads
    groups = []
    for head in range(0, heads, 4):
        low = head * head_dim
        base = low // LANES * LANES
        groups.append((head, base, low - base))
    return head_dim, groups


def token_fwd_kernel(query_ref, keyval_ref, bias_ref, attend_ref, probs_ref, fold_s):
    tokens, width = query_ref.shape[1:]
    heads = bias_ref.shape[0]
    keys = bias_ref.shape[2]
    head_dim, groups = head_groups(width, heads)
    scale = float(head_dim) ** (-0.5)
    fold_s[...] = jnp.zeros_like(fold_s)
    for head, base, first in groups:
        span = slice(base, base + 256)
        key_rows = keyval_ref[:, 0, :, base : base + 256].reshape(keys, 256)
        value_rows = keyval_ref[:, 0, :, width + base : width + base + 256].reshape(keys, 256)
        stacked = head_stack(query_ref[0, :, span], 4, head_dim, first)
        bias = bias_ref[head : head + 4].reshape(4 * tokens, keys)
        scores = mm_nt(stacked, key_rows) * scale + bias
        exp_scores = jnp.exp(scores - jnp.max(scores, -1, keepdims=True))
        probs = exp_scores * (1.0 / jnp.sum(exp_scores, -1, keepdims=True))
        probs_low = probs.astype(bf16)
        probs_ref[0, head : head + 4] = probs_low.reshape(4, tokens, keys)
        fold_s[:, span] += head_fold(mm(probs_low, value_rows), 4, head_dim, first)
    attend_ref[0] = fold_s[...]


def token_attention(query, keyval, bias):
    samples, tokens, width = query.shape
    heads, _, keys = bias.shape
    devices = keyval.shape[0]
    return pl.pallas_call(
        token_fwd_kernel,
        out_shape=[
            jax.ShapeDtypeStruct(query.shape, f32),
            jax.ShapeDtypeStruct((samples, heads, tokens, keys), bf16),
        ],
        grid=(samples,),
        in_specs=[
            per_sample((tokens, width)),
            pl.BlockSpec((devices, 1, tokens, 2 * width), lambda b: (0, b, 0, 0)),
            whole(bias.shape),
        ],
        out_specs=[per_sample((tokens, width)), per_sample((heads, tokens, keys))],
        scratch_shapes=[pltpu.VMEM((tokens, width), f32)],
        compiler_params=params(),
        name="token_attention",
    )(query, keyval, bias)


def token_bwd_kernel(
    query_ref, keyval_ref, probs_ref, att_ref, dq_ref, dkv_ref, bias_ref, fold_s, grad_s
):
    tokens, width = query_ref.shape[1:]
    heads, _, keys = bias_ref.shape
    devices = keyval_ref.shape[0]
    head_dim, groups = head_groups(width, heads)
    scale = float(head_dim) ** (-0.5)

    @pl.when(pl.program_id(0) == 0)
    def _():
        bias_ref[...] = jnp.zeros_like(bias_ref)

    fold_s[...] = jnp.zeros_like(fold_s)
    grad_s[...] = jnp.zeros_like(grad_s)
    for head, base, first in groups:
        span = slice(base, base + 256)
        key_rows = keyval_ref[:, 0, :, base : base + 256].reshape(keys, 256)
        value_rows = keyval_ref[:, 0, :, width + base : width + base + 256].reshape(keys, 256)
        queries = head_stack(query_ref[0, :, span], 4, head_dim, first)
        att = head_stack(att_ref[0, :, span], 4, head_dim, first)
        probs_low = probs_ref[0, head : head + 4].reshape(4 * tokens, keys)
        probs = probs_low.astype(f32)
        prob_grad = mm_nt(att, value_rows)
        delta = jnp.sum(prob_grad * probs, -1, keepdims=True)
        score_low = (probs * (prob_grad - delta)).astype(bf16)
        bias_ref[head : head + 4] += score_low.astype(f32).reshape(4, tokens, keys)
        fold_s[:, span] += head_fold(mm(score_low, key_rows), 4, head_dim, first) * scale
        grad_s[:, span] += mm_tn(score_low, queries) * scale
        grad_s[:, width + base : width + base + 256] += mm_tn(probs_low, att)
    dq_ref[0] = fold_s[...]
    dkv_ref[:, 0] = grad_s[...].astype(bf16).reshape(devices, tokens, 2 * width)


def token_attention_back(query, keyval, probs, att):
    samples, tokens, width = query.shape
    heads, _, keys = probs.shape[1:]
    devices = keyval.shape[0]
    return pl.pallas_call(
        token_bwd_kernel,
        out_shape=[
            jax.ShapeDtypeStruct(query.shape, f32),
            jax.ShapeDtypeStruct(keyval.shape, bf16),
            jax.ShapeDtypeStruct((heads, tokens, keys), f32),
        ],
        grid=(samples,),
        in_specs=[
            per_sample((tokens, width)),
            pl.BlockSpec((devices, 1, tokens, 2 * width), lambda b: (0, b, 0, 0)),
            per_sample((heads, tokens, keys)),
            per_sample((tokens, width)),
        ],
        out_specs=[
            per_sample((tokens, width)),
            pl.BlockSpec((devices, 1, tokens, 2 * width), lambda b: (0, b, 0, 0)),
            whole((heads, tokens, keys)),
        ],
        scratch_shapes=[
            pltpu.VMEM((tokens, width), f32),
            pltpu.VMEM((keys, 2 * width), f32),
        ],
        compiler_params=params(),
        name="token_attention_back",
    )(query, keyval, probs, att)


def token_open_kernel(
    noise,
    direction_ref,
    single_ref,
    pooled_ref,
    tokens_ref,
    condw_ref,
    condb_ref,
    proj_ref,
    qbias_ref,
    block_ref,
    condlow_ref,
    cond_ref,
    attn_ref,
    query_ref,
    keyval_ref,
    gating_ref,
):
    width = tokens_ref.shape[1]
    count = single_ref.shape[0]
    step = pl.program_id(0)
    single = single_ref[...].astype(f32)
    direction = direction_ref[...]
    for part in range(tokens_ref.shape[0] // count):
        level = jnp.full(direction.shape, noise[step * (tokens_ref.shape[0] // count) + part], f32)
        shifted = single + 0.25 * jnp.log(level / sigma_data) * direction
        condlow_ref[part * count : (part + 1) * count, :] = norm_stats(shifted)[0].astype(bf16)
    cond_low = condlow_ref[...]
    for part in range(6):
        lanes = slice(part * width, (part + 1) * width)
        cond_ref[:, lanes] = mm(cond_low, condw_ref[:, lanes]) + condb_ref[:, lanes]
    block_in = tokens_ref[...].astype(f32) + pooled_ref[...]
    block_ref[...] = block_in
    normed = norm_stats(block_in)[0]
    attn_in = (sigmoid(cond_ref[:, :width]) * normed + cond_ref[:, width : 2 * width]).astype(bf16)
    attn_ref[...] = attn_in
    query_ref[...] = (mm(attn_in, proj_ref[:, :width]) + qbias_ref[...]).astype(bf16)
    keyval_ref[...] = mm(attn_in, proj_ref[:, width : 3 * width]).astype(bf16)
    gating_ref[...] = mm(attn_in, proj_ref[:, 3 * width :])


def token_open(noise, direction, single, pooled, tokens, condw, condb, proj, qbias):
    samples, count, width = tokens.shape
    rows = samples * count
    block = 2 * count
    lanes = lambda size: pl.BlockSpec((block, size), lambda i: (i, 0))
    inner = single.shape[1]
    outs = (
        (width, f32),
        (inner, bf16),
        (6 * width, f32),
        (width, bf16),
        (width, bf16),
        (2 * width, bf16),
        (width, f32),
    )
    return pl.pallas_call(
        token_open_kernel,
        out_shape=[jax.ShapeDtypeStruct((rows, size), kind) for size, kind in outs],
        grid=(rows // block,),
        in_specs=[
            pl.BlockSpec(memory_space=pltpu.SMEM),
            whole((1, inner)),
            whole(single.shape),
            lanes(width),
            lanes(width),
            whole(condw.shape),
            whole((1, 6 * width)),
            whole(proj.shape),
            whole((1, width)),
        ],
        out_specs=[lanes(size) for size, _ in outs],
        compiler_params=params(),
        name="token_open",
    )(
        noise,
        direction.reshape(1, -1),
        single,
        pooled.reshape(rows, width),
        tokens.reshape(rows, width),
        condw,
        condb.reshape(1, -1),
        proj,
        qbias.reshape(1, -1),
    )


def token_middle_rows(
    attend,
    gating_ref,
    block_ref,
    gate1_ref,
    scale2_ref,
    shift2_ref,
    gate2_ref,
    cotangent_ref,
    outw_ref,
    upw_ref,
    downw_ref,
    result_ref,
    ffn_ref,
    upper_ref,
    hidden_ref,
    two_ref,
    gated_ref,
    branch_ref,
    att_ref,
    gategrad_ref,
    midgrad_ref,
    condgrad_ref,
):
    width = attend.shape[1]
    hidden_width = downw_ref.shape[0]
    outw, upw, downw = outw_ref[...], upw_ref[...], downw_ref[...]
    sig_gate = sigmoid(gating_ref[...])
    gated_low = (attend * sig_gate).astype(bf16)
    gated_ref[...] = gated_low
    branch = mm(gated_low, outw)
    gate_one = sigmoid(gate1_ref[...])
    mid = block_ref[...] + gate_one * branch
    normed, inv_std = norm_stats(mid)
    scale_two = sigmoid(scale2_ref[...])
    ffn_in = (scale_two * normed + shift2_ref[...]).astype(bf16)
    ffn_ref[...] = ffn_in
    first_half = mm(ffn_in, upw[:, :hidden_width])
    second_half = mm(ffn_in, upw[:, hidden_width:])
    sig_first = sigmoid(first_half)
    hidden = (first_half * sig_first * second_half).astype(bf16)
    hidden_ref[...] = hidden
    branch_two = mm(hidden, downw)
    gate_two = sigmoid(gate2_ref[...])
    result_ref[...] = (mid + gate_two * branch_two).astype(bf16)

    out_grad = cotangent_ref[...].astype(f32)
    two_low = (out_grad * gate_two).astype(bf16)
    two_ref[...] = two_low
    condgrad_ref[:, 3 * width :] = (
        out_grad * branch_two * gate_two * (1.0 - gate_two)
    ).astype(bf16)
    hidden_grad = mm_nt(two_low, downw)
    first_grad = (
        hidden_grad * second_half * sig_first * (1.0 + first_half * (1.0 - sig_first))
    ).astype(bf16)
    second_grad = (hidden_grad * first_half * sig_first).astype(bf16)
    upper_ref[:, :hidden_width] = first_grad
    upper_ref[:, hidden_width:] = second_grad
    ffn_grad = mm_nt(first_grad, upw[:, :hidden_width]) + mm_nt(second_grad, upw[:, hidden_width:])
    condgrad_ref[:, 2 * width : 3 * width] = ffn_grad.astype(bf16)
    condgrad_ref[:, width : 2 * width] = (
        ffn_grad * normed * scale_two * (1.0 - scale_two)
    ).astype(bf16)
    mid_grad = out_grad + norm_back(normed, inv_std, ffn_grad * scale_two)
    midgrad_ref[...] = mid_grad
    branch_low = (mid_grad * gate_one).astype(bf16)
    branch_ref[...] = branch_low
    condgrad_ref[:, :width] = (mid_grad * branch * gate_one * (1.0 - gate_one)).astype(bf16)
    gated_grad = mm_nt(branch_low, outw)
    att_ref[...] = (gated_grad * sig_gate).astype(bf16)
    gategrad_ref[...] = (gated_grad * attend * sig_gate * (1.0 - sig_gate)).astype(bf16)


def attend_groups(heads, width, tokens, query, keyval, bias, probs_ref, fold_s):
    head_dim, groups = head_groups(width, heads)
    scale = float(head_dim) ** (-0.5)
    fold_s[...] = jnp.zeros_like(fold_s)
    for head, base, first in groups:
        span = slice(base, base + 256)
        stacked = head_stack(query[:, span], 4, head_dim, first)
        scores = mm_nt(stacked, keyval(base)) * scale + bias(head)
        exp_scores = jnp.exp(scores - jnp.max(scores, -1, keepdims=True))
        probs = exp_scores * (1.0 / jnp.sum(exp_scores, -1, keepdims=True))
        probs_low = probs.astype(bf16)
        probs_ref[0, head : head + 4] = probs_low.reshape(4, tokens, -1)
        fold_s[:, span] += head_fold(mm(probs_low, keyval(width + base)), 4, head_dim, first)


def gather_attend_kernel(
    query_ref,
    own_ref,
    pair_ref,
    weight_ref,
    gating_ref,
    block_ref,
    gate1_ref,
    scale2_ref,
    shift2_ref,
    gate2_ref,
    cotangent_ref,
    outw_ref,
    upw_ref,
    downw_ref,
    probs_ref,
    keyval_ref,
    stats_ref,
    *refs,
):
    middle, (all_s, bias_s, fold_s, attend_s, send, recv, load) = refs[:11], refs[11:]
    z, me, sib, xn, yn, dg = places()
    step = pl.program_id(0)
    tokens, width = query_ref.shape[1:]
    heads = weight_ref.shape[0]
    devices, samples = all_s.shape[:2]
    keys = devices * tokens
    head, tail, full = slice(0, width), slice(width, 2 * width), slice(0, 2 * width)

    def unit(part, sample, lanes, kind, device):
        ref = all_s.at[part, sample, :, lanes]
        return remote(ref, ref, send.at[kind, sample], recv.at[kind, sample], (z, device))

    def issue(sample):
        unit(me, sample, full, 0, xn).start()
        unit(me, sample, full, 1, yn).start()
        unit(me, sample, full, 4, sib).start()

    def relay(sample):
        unit(xn, sample, full, 0, xn).wait_recv()
        unit(xn, sample, head, 2, yn).start()
        unit(xn, sample, full, 5, sib).start()
        unit(yn, sample, full, 1, yn).wait_recv()
        unit(yn, sample, tail, 3, xn).start()
        unit(yn, sample, full, 6, sib).start()

    def collect(sample):
        unit(dg, sample, head, 2, yn).wait_recv()
        unit(dg, sample, tail, 3, xn).wait_recv()
        unit(dg, sample, full, 7, sib).start()

    @pl.when(step == 0)
    def _():
        copy = pltpu.make_async_copy(own_ref, all_s.at[me], load)
        copy.start()
        greet([(z, sib), (z, xn), (z, yn)])
        copy.wait()
        issue(0)
        issue(1)

    @pl.when((step >= 1) & (step - 1 < samples))
    def _():
        relay(step - 1)

    @pl.when((step >= 1) & (step + 1 < samples))
    def _():
        issue(step + 1)

    @pl.when((step >= 2) & (step - 2 < samples))
    def _():
        collect(step - 2)

    @pl.when(step < 2)
    def _():
        weights = weight_ref[...]
        ones_op = jnp.ones((16, weights.shape[1]), bf16)
        weight_sum = jnp.sum(weights.astype(f32), -1, keepdims=True)
        groups = pair_ref.shape[0] // 8

        def one(group, carry):
            for row in range(8):
                product, mean, inv_std = row_stats(pair_ref[group * 8 + row], ones_op, weights)
                place = step * groups + group
                bias_s[:, place, row, :] = inv_std * (product - mean * weight_sum)
                stats_ref[0, place, row : row + 1, :] = mean
                stats_ref[1, place, row : row + 1, :] = inv_std
            return carry

        lax.fori_loop(0, groups, one, 0)

    @pl.when(step >= 3)
    def _():
        sample = step - 3
        for kind, part in ((4, sib), (5, sib), (6, sib), (7, sib)):
            unit(part, sample, full, kind, sib).wait_recv()
        for part in range(devices):
            keyval_ref[part, 0] = all_s[part, sample]
        attend_groups(
            heads,
            width,
            tokens,
            query_ref[0],
            lambda base: keyval_ref[:, 0, :, base : base + 256].reshape(keys, 256),
            lambda head: bias_s[head : head + 4].reshape(4 * tokens, keys),
            probs_ref,
            fold_s,
        )
        attend_s[pl.ds(pl.multiple_of(sample % 2 * tokens, 16), tokens), :] = fold_s[...]

    @pl.when((step >= 3) & (step % 2 == 0))
    def _():
        token_middle_rows(
            attend_s[...],
            gating_ref,
            block_ref,
            gate1_ref,
            scale2_ref,
            shift2_ref,
            gate2_ref,
            cotangent_ref,
            outw_ref,
            upw_ref,
            downw_ref,
            *middle,
        )

    @pl.when(step == pl.num_programs(0) - 1)
    def _():
        def sent(sample, carry):
            for kind in (0, 1, 4, 5, 6, 7):
                unit(me, sample, full, kind, sib).wait_send()
            unit(me, sample, head, 2, sib).wait_send()
            unit(me, sample, tail, 3, sib).wait_send()
            return carry

        lax.fori_loop(0, samples, sent, 0)


def held_once(shape):
    return pl.BlockSpec(shape, lambda *_: (0,) * len(shape), pipeline_mode=pl.Buffered(1))


def gather_attend(
    query, own, pairs, weights, gating, block_in, cond_all, cotangent, outw, upw, downw
):
    samples, tokens, width = query.shape
    heads, features = weights.shape
    seq = lax.axis_size("seq")
    keys = seq * tokens
    hidden_width = downw.shape[0]
    rows, block = samples * tokens, 2 * tokens
    late = lambda g: jnp.maximum(g - 3, 0)
    sample_block = lambda shape: pl.BlockSpec((1,) + shape, lambda g: (late(g),) + (0,) * len(shape))
    duo_block = lambda lanes, column=0: pl.BlockSpec((block, lanes), lambda g: (late(g) // 2, column))
    flat = lambda part: part.reshape(rows, part.shape[-1])
    cond = flat(cond_all)
    dma = pltpu.SemaphoreType.DMA
    outs = (
        (width, bf16),
        (width, bf16),
        (2 * hidden_width, bf16),
        (hidden_width, bf16),
        (width, bf16),
        (width, bf16),
        (width, bf16),
        (width, bf16),
        (width, bf16),
        (width, f32),
        (4 * width, bf16),
    )
    results = pl.pallas_call(
        gather_attend_kernel,
        out_shape=[
            jax.ShapeDtypeStruct((samples, heads, tokens, keys), bf16),
            jax.ShapeDtypeStruct((seq, samples, tokens, 2 * width), bf16),
            jax.ShapeDtypeStruct((2, tokens // 8, 8, keys), f32),
        ]
        + [jax.ShapeDtypeStruct((rows, lanes), kind) for lanes, kind in outs],
        grid=(samples + 3,),
        in_specs=[
            sample_block((tokens, width)),
            pl.BlockSpec(memory_space=pl.ANY),
            pl.BlockSpec((tokens // 2, keys, features), lambda g: (jnp.minimum(g, 1), 0, 0)),
            whole(weights.shape),
            duo_block(width),
            duo_block(width),
            duo_block(width, 2),
            duo_block(width, 3),
            duo_block(width, 4),
            duo_block(width, 5),
            duo_block(width),
        ]
        + [held_once(part.shape) for part in (outw, upw, downw)],
        out_specs=[
            sample_block((heads, tokens, keys)),
            pl.BlockSpec((seq, 1, tokens, 2 * width), lambda g: (0, late(g), 0, 0)),
            whole((2, tokens // 8, 8, keys)),
        ]
        + [duo_block(lanes) for lanes, _ in outs],
        scratch_shapes=[
            pltpu.VMEM((seq, samples, tokens, 2 * width), bf16),
            pltpu.VMEM((heads, tokens // 8, 8, keys), f32),
            pltpu.VMEM((tokens, width), f32),
            pltpu.VMEM((block, width), f32),
            dma((8, samples)),
            dma((8, samples)),
            dma,
        ],
        compiler_params=pltpu.CompilerParams(
            vmem_limit_bytes=60 << 20, collective_id=4, has_side_effects=True
        ),
        name="gather_attend",
    )(
        query,
        own,
        pairs,
        weights,
        flat(gating),
        flat(block_in),
        cond,
        cond,
        cond,
        cond,
        flat(cotangent),
        outw,
        upw,
        downw,
    )
    return results[:3], results[3:]


def attend_back_scatter_kernel(
    query_ref,
    keyval_ref,
    probs_ref,
    att_ref,
    pair_ref,
    stats_ref,
    ffn_ref,
    upper_ref,
    hidden_ref,
    two_ref,
    gated_ref,
    branch_ref,
    dq_ref,
    dkv_ref,
    pairw_ref,
    pairm_ref,
    upw_ref,
    downw_ref,
    outw_ref,
    fold_s,
    grad_s,
    bias_s,
    mine,
    theirs,
    from_x,
    from_y,
    last_x,
    last_y,
    s_sib,
    r_sib,
    s_one,
    r_one,
    s_two,
    r_two,
):
    z, me, sib, xn, yn, dg = places()
    core, chip = me % 2, me // 2
    chip_x, chip_y, chip_d = xn // 2, yn // 2, dg // 2
    step = pl.program_id(0)
    tokens, width = query_ref.shape[1:]
    samples = mine.shape[0]
    heads, keys = probs_ref.shape[1], probs_ref.shape[3]
    head_dim, groups = head_groups(width, heads)
    scale = float(head_dim) ** (-0.5)
    head, tail = slice(0, width), slice(width, 2 * width)

    def there(b):
        return remote(
            mine.at[b, :, 1 - core], theirs.at[b], s_sib.at[b], r_sib.at[b], (z, sib)
        )

    def one(b, k):
        part = (chip_x, chip_d, chip_y, chip_d)[k]
        lanes = head if k < 2 else tail
        target = (from_x if k < 2 else from_y).at[b, k % 2]
        device = xn if k < 2 else yn
        source = mine.at[b, part, core, :, lanes]
        return remote(source, target, s_one.at[b, k], r_one.at[b, k], (z, device))

    def two(b, k):
        part, lanes, target, device = ((chip_y, head, last_y, yn), (chip_x, tail, last_x, xn))[k]
        source = mine.at[b, part, core, :, lanes]
        return remote(source, target.at[b], s_two.at[b, k], r_two.at[b, k], (z, device))

    def add(b, part, lanes, source):
        both = mine[b, part, core, :, lanes].astype(f32) + source.astype(f32)
        mine[b, part, core, :, lanes] = both.astype(bf16)

    @pl.when(step == 0)
    def _():
        greet([(z, sib), (z, xn), (z, yn)])
        bias_s[...] = jnp.zeros_like(bias_s)
        pairw_ref[...] = jnp.zeros_like(pairw_ref)
        pairm_ref[...] = jnp.zeros_like(pairm_ref)

    @pl.when((step >= 1) & (step - 1 < samples))
    def _():
        b = step - 1
        there(b).wait_recv()

        def chips(j, carry):
            add(b, j, slice(0, 2 * width), theirs[b, j])
            return carry

        lax.fori_loop(0, 4, chips, 0)
        for k in range(4):
            one(b, k).start()

    @pl.when((step >= 2) & (step - 2 < samples))
    def _():
        b = step - 2
        one(b, 1).wait_recv()
        add(b, chip_y, head, from_x[b, 1])
        two(b, 0).start()
        one(b, 3).wait_recv()
        add(b, chip_x, tail, from_y[b, 1])
        two(b, 1).start()
        one(b, 0).wait_recv()
        add(b, chip, head, from_x[b, 0])
        one(b, 2).wait_recv()
        add(b, chip, tail, from_y[b, 0])

    @pl.when((step >= 3) & (step - 3 < samples))
    def _():
        b = step - 3
        two(b, 0).wait_recv()
        add(b, chip, head, last_y[b])
        two(b, 1).wait_recv()
        add(b, chip, tail, last_x[b])
        dkv_ref[0] = mine[b, chip, core]

    @pl.when(step < samples)
    def _():
        fold_s[...] = jnp.zeros_like(fold_s)
        grad_s[...] = jnp.zeros_like(grad_s)
        for first_head, base, first in groups:
            span = slice(base, base + 256)
            key_rows = keyval_ref[:, 0, :, base : base + 256].reshape(keys, 256)
            value_rows = keyval_ref[:, 0, :, width + base : width + base + 256].reshape(keys, 256)
            queries = head_stack(query_ref[0, :, span], 4, head_dim, first)
            att = head_stack(att_ref[0, :, span], 4, head_dim, first)
            probs_low = probs_ref[0, first_head : first_head + 4].reshape(4 * tokens, keys)
            probs = probs_low.astype(f32)
            prob_grad = mm_nt(att, value_rows)
            delta = jnp.sum(prob_grad * probs, -1, keepdims=True)
            score_low = (probs * (prob_grad - delta)).astype(bf16)
            bias_s[first_head : first_head + 4] += score_low.astype(f32).reshape(
                4, tokens // 8, 8, keys
            )
            fold_s[:, span] += head_fold(mm(score_low, key_rows), 4, head_dim, first) * scale
            grad_s[:, span] += mm_tn(score_low, queries) * scale
            grad_s[:, width + base : width + base + 256] += mm_tn(probs_low, att)
        dq_ref[0] = fold_s[...]
        mine[step] = grad_s[...].astype(bf16).reshape(mine.shape[1:])
        there(step).start()
        upw_ref[...] = mm_tn(ffn_ref[...], upper_ref[...]).astype(bf16)

    @pl.when(step < 6)
    def _():
        downw_ref[...] = mm_tn(hidden_ref[...], two_ref[...]).astype(bf16)

    @pl.when((step >= 6) & (step < 8))
    def _():
        outw_ref[...] = mm_tn(gated_ref[...], branch_ref[...]).astype(bf16)

    @pl.when((step >= samples) & (step < samples + 2))
    def _():
        rows = pair_ref.shape[0] // 8

        def some(group, carry):
            total, means = carry
            place = (step - samples) * rows + group
            for row in range(8):
                inv_std = stats_ref[1, place, row : row + 1, :]
                scaled = bias_s[:, place, row, :] * inv_std
                means += scaled * stats_ref[0, place, row : row + 1, :]
                upper = scaled.astype(bf16)
                lower = (scaled - upper.astype(f32)).astype(bf16)
                both = mm(jnp.concatenate([upper, lower], 0), pair_ref[group * 8 + row])
                total += both[:heads] + both[heads:]
            return total, means

        zeros = (jnp.zeros(pairw_ref.shape, f32), jnp.zeros(pairm_ref.shape, f32))
        total, means = lax.fori_loop(0, rows, some, zeros)
        pairw_ref[...] += total
        pairm_ref[...] += means

    @pl.when(step == pl.num_programs(0) - 1)
    def _():
        def sent(b, carry):
            there(b).wait_send()
            for k in range(4):
                one(b, k).wait_send()
            for k in range(2):
                two(b, k).wait_send()
            return carry

        lax.fori_loop(0, samples, sent, 0)


def attend_back_scatter(query, keyval, probs, att, pairs, stats, ffn, upper, hidden, two, gated, branch):
    samples, tokens, width = query.shape
    heads, _, keys = probs.shape[1:]
    seq = keyval.shape[0]
    features = pairs.shape[-1]
    flat = [part.reshape(-1, part.shape[-1]) for part in (ffn, upper, hidden, two, gated, branch)]
    rows = flat[0].shape[0]
    held = lambda g: jnp.minimum(g, samples - 1)
    late = lambda g: jnp.clip(g - 3, 0, samples - 1)
    pair_step = lambda g: jnp.clip(g - samples, 0, 1)
    up_step = lambda g: jnp.minimum(g, seq - 1)
    down_step = lambda g: jnp.minimum(g, 5)
    out_step = lambda g: jnp.clip(g - 6, 0, 1)
    sample_block = lambda shape, at: pl.BlockSpec((1,) + shape, lambda g: (at(g),) + (0,) * len(shape))
    keyval_block = pl.BlockSpec((seq, 1, tokens, 2 * width), lambda g: (0, held(g), 0, 0))
    up_width = flat[1].shape[1] // seq
    hidden_width = flat[2].shape[1]
    dma = pltpu.SemaphoreType.DMA
    results = pl.pallas_call(
        attend_back_scatter_kernel,
        out_shape=[
            jax.ShapeDtypeStruct(query.shape, f32),
            jax.ShapeDtypeStruct((samples, tokens, 2 * width), bf16),
            jax.ShapeDtypeStruct((heads, features), f32),
            jax.ShapeDtypeStruct((heads, keys), f32),
            jax.ShapeDtypeStruct((width, flat[1].shape[1]), bf16),
            jax.ShapeDtypeStruct((hidden_width, width), bf16),
            jax.ShapeDtypeStruct((width, width), bf16),
        ],
        grid=(samples + 3,),
        in_specs=[
            sample_block((tokens, width), held),
            keyval_block,
            sample_block((heads, tokens, keys), held),
            sample_block((tokens, width), held),
            pl.BlockSpec((tokens // 2, keys, features), lambda g: (pair_step(g), 0, 0)),
            whole(stats.shape),
            whole(flat[0].shape),
            pl.BlockSpec((rows, up_width), lambda g: (0, up_step(g))),
            pl.BlockSpec((rows, 256), lambda g: (0, down_step(g))),
            whole(flat[3].shape),
            pl.BlockSpec((rows, width // 2), lambda g: (0, out_step(g))),
            whole(flat[5].shape),
        ],
        out_specs=[
            sample_block((tokens, width), held),
            sample_block((tokens, 2 * width), late),
            whole((heads, features)),
            whole((heads, keys)),
            pl.BlockSpec((width, up_width), lambda g: (0, up_step(g))),
            pl.BlockSpec((256, width), lambda g: (down_step(g), 0)),
            pl.BlockSpec((width // 2, width), lambda g: (out_step(g), 0)),
        ],
        scratch_shapes=[
            pltpu.VMEM((tokens, width), f32),
            pltpu.VMEM((keys, 2 * width), f32),
            pltpu.VMEM((heads, tokens // 8, 8, keys), f32),
            pltpu.VMEM((samples, seq // 2, 2, tokens, 2 * width), bf16),
            pltpu.VMEM((samples, seq // 2, tokens, 2 * width), bf16),
            pltpu.VMEM((samples, 2, tokens, width), bf16),
            pltpu.VMEM((samples, 2, tokens, width), bf16),
            pltpu.VMEM((samples, tokens, width), bf16),
            pltpu.VMEM((samples, tokens, width), bf16),
            dma((samples,)),
            dma((samples,)),
            dma((samples, 4)),
            dma((samples, 4)),
            dma((samples, 2)),
            dma((samples, 2)),
        ],
        compiler_params=pltpu.CompilerParams(
            vmem_limit_bytes=60 << 20, collective_id=5, has_side_effects=True
        ),
        name="attend_back_scatter",
    )(query, keyval, probs, att, pairs, stats, *flat)
    dq, dkv, total, means, upw, downw, outw = results
    return dq, dkv, total - jnp.sum(means, -1, keepdims=True), (upw, downw, outw)


def token_close_kernel(
    dq_ref,
    dkv_ref,
    gategrad_ref,
    midgrad_ref,
    block_ref,
    scale1_ref,
    tail_ref,
    proj_ref,
    attn_ref,
    cond_ref,
    upw_ref,
    downw_ref,
    outw_ref,
    tokengrad_ref,
    qbias_ref,
    cbias_ref,
    units_ref,
    mix_s,
    condgrad_s,
    cond_s,
    proj_s,
):
    step = pl.program_id(0)
    block, width = dq_ref.shape
    blocks = mix_s.shape[0] // block
    samp = units_ref.shape[1]

    @pl.when(step == 0)
    def _():
        qbias_ref[...] = jnp.zeros_like(qbias_ref)
        cbias_ref[...] = jnp.zeros_like(cbias_ref)

    @pl.when(step < blocks)
    def _():
        rows = pl.ds(pl.multiple_of(step * block, block), block)
        dq = dq_ref[...]
        qbias_ref[...] += jnp.sum(dq, 0, keepdims=True)
        mix = jnp.concatenate([dq.astype(bf16), dkv_ref[...], gategrad_ref[...]], 1)
        mix_s[rows, :] = mix
        attn_grad = mm_nt(mix, proj_ref[...])
        normed, inv_std = norm_stats(block_ref[...])
        scale_one = sigmoid(scale1_ref[...])
        scale_grad = (attn_grad * normed * scale_one * (1.0 - scale_one)).astype(bf16)
        tokengrad_ref[...] = midgrad_ref[...] + norm_back(normed, inv_std, attn_grad * scale_one)
        shift_grad = attn_grad.astype(bf16)
        tail = tail_ref[...]
        condgrad_s[rows, :width] = scale_grad
        condgrad_s[rows, width : 2 * width] = shift_grad
        condgrad_s[rows, 2 * width :] = tail
        for part, low in ((scale_grad, 0), (shift_grad, width), (tail, 2 * width)):
            cbias_ref[:, low : low + part.shape[1]] += jnp.sum(
                part.astype(f32), 0, keepdims=True
            )

    @pl.when(step == blocks)
    def _():
        cond_rows = cond_ref[...].T
        for low in range(0, cond_s.shape[1], 768):
            cond_s[:, low : low + 768] = mm(cond_rows, condgrad_s[:, low : low + 768]).astype(bf16)
        attn_rows = attn_ref[...].T
        for low in range(0, proj_s.shape[1], 768):
            proj_s[:, low : low + 768] = mm(attn_rows, mix_s[:, low : low + 768]).astype(bf16)

    @pl.when(step >= blocks)
    def _():
        part = step - blocks
        left = pl.multiple_of(part * 384, LANES)
        proj = proj_s[:, pl.ds(left, 384)]
        rows = proj.shape[0] // samp
        for z in range(samp):
            units_ref[0, z, :rows, :384] = proj[z * rows : (z + 1) * rows]
            units_ref[0, z, :rows, 384:] = upw_ref[z * rows : (z + 1) * rows, :]
            units_ref[0, z, 192:240, :] = downw_ref[
                pl.ds(pl.multiple_of(z * 384 + part * 48, 16), 48), :
            ]
            low = pl.multiple_of(z * 96 + part // 4 * 48, 16)
            left = pl.multiple_of(part % 4 * 1152, LANES)
            units_ref[0, z, 240:288, :] = cond_s[pl.ds(low, 48), pl.ds(left, 768)]
            left = pl.multiple_of(part % 4 * 1152 + 768, LANES)
            units_ref[0, z, 288:336, :384] = cond_s[pl.ds(low, 48), pl.ds(left, 384)]
            low = pl.multiple_of(z * 192 + part // 2 * 48, 16)
            left = pl.multiple_of(part % 2 * 384, LANES)
            units_ref[0, z, 288:336, 384:] = outw_ref[pl.ds(low, 48), pl.ds(left, 384)]


def token_close(dq, dkv, gategrad, midgrad, block_in, cond_all, tail, proj, attn_in, cond_low, ready, samp, seq):
    samples, tokens, width = dq.shape
    rows = samples * tokens
    blocks = 4
    block = rows // blocks
    flat = lambda part: part.reshape(rows, part.shape[-1])
    upw, downw, outw = ready
    attn, cond = flat(attn_in), flat(cond_low)

    def early(lanes, column=0):
        return pl.BlockSpec((block, lanes), lambda g: (jnp.minimum(g, blocks - 1), column))

    late = lambda g: jnp.maximum(g - blocks, 0)
    return pl.pallas_call(
        token_close_kernel,
        out_shape=[
            jax.ShapeDtypeStruct((rows, width), f32),
            jax.ShapeDtypeStruct((1, width), f32),
            jax.ShapeDtypeStruct((1, 6 * width), f32),
            jax.ShapeDtypeStruct((seq, samp, UNIT, 768), bf16),
        ],
        grid=(blocks + seq,),
        in_specs=[
            early(width),
            early(2 * width),
            early(width),
            early(width),
            early(width),
            early(width),
            early(4 * width),
            whole(proj.shape),
            whole(attn.shape),
            whole(cond.shape),
            pl.BlockSpec((width, 384), lambda g: (0, late(g))),
            whole(downw.shape),
            whole(outw.shape),
        ],
        out_specs=[
            early(width),
            whole((1, width)),
            whole((1, 6 * width)),
            pl.BlockSpec((1, samp, UNIT, 768), lambda g: (late(g), 0, 0, 0)),
        ],
        scratch_shapes=[
            pltpu.VMEM((rows, 4 * width), bf16),
            pltpu.VMEM((rows, 6 * width), bf16),
            pltpu.VMEM((cond.shape[1], 6 * width), bf16),
            pltpu.VMEM((width, 4 * width), bf16),
        ],
        compiler_params=params(),
        name="token_close",
    )(
        flat(dq),
        flat(dkv),
        gategrad,
        midgrad,
        flat(block_in),
        flat(cond_all),
        tail,
        proj,
        attn,
        cond,
        upw,
        downw,
        outw,
    )


def to_blocks(array, width):
    return [array[:, low : low + width] for low in range(0, array.shape[1], width)]


def pack_blocks(arrays, width):
    parts = []
    for array in arrays:
        parts += to_blocks(array, width)
    return jnp.concatenate(parts, 0)


def unpack_blocks(packed, shapes, width):
    arrays, low = [], 0
    for rows, columns in shapes:
        parts = []
        for _ in range(columns // width):
            parts.append(packed[low : low + rows])
            low += rows
        arrays.append(jnp.concatenate(parts, 1) if len(parts) > 1 else parts[0])
    return arrays


def sum_shares(grads, extra):
    samp, seq = lax.axis_size("samp"), lax.axis_size("seq")
    width = grads[2].shape[1]
    shapes = [(grad.shape[0] // samp, grad.shape[1]) for grad in grads]
    packed = jnp.concatenate(
        [
            block.astype(bf16).reshape(samp, -1, width)
            for grad in grads
            for block in to_blocks(grad, width)
        ]
        + [extra.astype(bf16).reshape(samp, -1, width)],
        1,
    )
    rows = packed.shape[1]
    packed = packed.reshape(samp, seq, rows // seq, width).transpose(1, 0, 2, 3)
    part = lax.psum_scatter(packed, "seq", scatter_dimension=0, tiled=False)
    part = lax.psum_scatter(part, "samp", scatter_dimension=0, tiled=False)
    packed = lax.all_gather(part, "seq", axis=0, tiled=True).astype(f32)
    shares = unpack_blocks(packed, shapes, width)
    return shares, packed[sum(r * (c // width) for r, c in shapes) :]


def local(
    atom_input,
    token_input,
    atom_counts,
    key_offsets,
    atom_pairs,
    pair_features,
    single_features,
    noise_levels,
    noise_direction,
    atom_proj,
    atom_qbias,
    atom_pairw,
    atom_outw,
    atom_upw,
    atom_downw,
    pool_weight,
    cond_weight,
    cond_bias,
    token_proj,
    token_qbias,
    token_pairw,
    token_outw,
    token_upw,
    token_downw,
    cotangent,
):
    samp, seq = lax.axis_size("samp"), lax.axis_size("seq")
    seq_pos = lax.axis_index("seq")
    samples, slots, atom_width = atom_input.shape
    tokens, width = token_input.shape[1:]
    features = atom_pairs.shape[-1]

    tiny_own = jnp.concatenate(
        [
            atom_qbias,
            cond_bias,
            token_qbias,
            atom_pairw.reshape(-1),
            token_pairw.reshape(-1),
        ]
    )
    tiny_own = jnp.pad(tiny_own, (0, -tiny_own.size % (16 * LANES))).reshape(-1, LANES)
    large = (token_proj, token_upw, token_downw, cond_weight, token_outw)
    kernels = samples == 8 and WeightGather.fits([part.shape for part in large], samp, seq)
    up_pairs = [(i, i + 1) for i in range(seq - 1)]
    down_pairs = [(i + 1, i) for i in range(seq - 1)]
    if kernels:
        wide, down, tiny_all, ext = edges(
            (atom_proj, atom_upw, pool_weight, atom_outw, atom_downw), tiny_own, atom_input
        )
    else:
        wide_own = jnp.concatenate([atom_proj, atom_upw, pool_weight, atom_outw], 1)
        wide = lax.all_gather(wide_own, "samp", axis=0, tiled=True)
        down = lax.all_gather(atom_downw, "samp", axis=0, tiled=True)
        tiny_all = lax.all_gather(tiny_own, "samp", axis=0, tiled=True)
        before = lax.ppermute(atom_input[:, slots - RIM :], "seq", up_pairs)
        after = lax.ppermute(atom_input[:, :RIM], "seq", down_pairs)
        ext = jnp.concatenate([before, atom_input, after], 1)
    tiny_all = tiny_all.reshape(samp, -1)
    sizes = [atom_qbias.size, cond_bias.size, token_qbias.size, atom_pairw.size, token_pairw.size]
    cuts = [sum(sizes[:i]) for i in range(6)]
    tiny = [tiny_all[:, cuts[i] : cuts[i + 1]] for i in range(5)]
    atom_qb = tiny[0].reshape(1, -1).astype(f32)
    cond_b = tiny[1].reshape(-1)
    token_qb = tiny[2].reshape(-1)
    atom_pw = tiny[3].reshape(features, ATOM_HEADS)
    token_pw = tiny[4].reshape(-1, token_pairw.shape[1])

    rim_tokens = RIM // MAX_ATOMS
    counts = lax.dynamic_slice_in_dim(
        jnp.pad(atom_counts, (rim_tokens, rim_tokens)), seq_pos * tokens, tokens + 2 * rim_tokens
    )
    place = jnp.arange(MAX_ATOMS, dtype=jnp.int32)
    used = place[None, :] < counts[:, None]
    blocked = jnp.where(used, 0.0, masked_score).astype(f32).reshape(-1, 1)
    blocked = jnp.broadcast_to(blocked, (blocked.shape[0], LANES))
    own_counts = counts[rim_tokens : rim_tokens + tokens]
    share = used[rim_tokens : rim_tokens + tokens].astype(f32) / own_counts[:, None].astype(f32)
    share = jnp.broadcast_to(share.reshape(-1, 1), (slots, LANES))
    windows = slots // WIN_Q
    starts = jnp.arange(windows, dtype=jnp.int32) * WIN_Q + key_offsets + RIM
    pairs_t = atom_pairs.transpose(0, 1, 3, 2).reshape(windows, WIN_Q * features, WIN_K)
    eye = jnp.eye(WIN_Q, dtype=bool)
    spread = jnp.where(
        eye[None, :, :, None], atom_pw.T[:, None, None, :], jnp.zeros((), bf16)
    ).reshape(ATOM_HEADS * WIN_Q, WIN_Q * features)
    gather = WeightGather([part.shape for part in large], samp, seq) if kernels else None
    pooled, stored, fulls = atom_forward(
        ext,
        starts,
        pairs_t,
        spread,
        blocked,
        share,
        wide,
        down,
        atom_qb,
        gather,
        large if kernels else (),
    )
    if not kernels:
        fulls = [lax.all_gather(part, "samp", axis=0, tiled=True) for part in large]
    proj_w, up_w, down_w, cond_w, out_w = fulls
    pair_w = token_pw.T
    if kernels:
        block_in, cond_low, cond_all, attn_in, queries, keyval_own, gating = token_open(
            noise_levels,
            noise_direction,
            single_features,
            pooled,
            token_input,
            cond_w,
            cond_b.astype(f32),
            proj_w,
            token_qb.astype(f32),
        )
        queries = queries.reshape(token_input.shape)
        keyval_own = keyval_own.reshape(samples, tokens, 2 * width)
    else:
        block_in = token_input.astype(f32) + pooled

        noise_feature = 0.25 * jnp.log(noise_levels / sigma_data)
        cond_rows = (
            single_features.astype(f32)[None]
            + noise_feature[:, None, None] * noise_direction[None, None, :]
        )
        cond_low = norm_stats(cond_rows)[0].astype(bf16)
        cond_all = dot_last(cond_low, cond_w) + cond_b.astype(f32)
        parts = [cond_all[..., i * width : (i + 1) * width] for i in range(6)]

        normed_in, inv_in = norm_stats(block_in)
        attn_in = (jax.nn.sigmoid(parts[0]) * normed_in + parts[1]).astype(bf16)
        mix = dot_last(attn_in, proj_w)
        queries = (mix[..., :width] + token_qb.astype(f32)).astype(bf16)
        keyval_own = mix[..., width : 3 * width].astype(bf16)
        gating = mix[..., 3 * width :]

    if kernels:
        (probs, keyval, stats), rows_out = gather_attend(
            queries,
            keyval_own,
            pair_features,
            pair_w,
            gating,
            block_in,
            cond_all,
            cotangent,
            out_w,
            up_w,
            down_w,
        )
        (
            block_out,
            ffn_in,
            upper_grad,
            hidden,
            branch_two_low,
            gated_low,
            branch_low,
            attend_low,
            gating_grad,
            mid_grad,
            cond_tail,
        ) = rows_out
        query_grad, keyval_grad, pairw_grad, ready = attend_back_scatter(
            queries,
            keyval,
            probs,
            attend_low.reshape(queries.shape),
            pair_features,
            stats,
            ffn_in,
            upper_grad,
            hidden,
            branch_two_low,
            gated_low,
            branch_low,
        )
        token_grad, token_qb_grad, cond_b_grad, grad_units = token_close(
            query_grad,
            keyval_grad,
            gating_grad,
            mid_grad,
            block_in,
            cond_all,
            cond_tail,
            proj_w,
            attn_in,
            cond_low,
            ready,
            samp,
            seq,
        )
        block_out = block_out.reshape(token_input.shape)
        token_grad = token_grad.reshape(token_input.shape)
        token_qb_grad, cond_b_grad = token_qb_grad.reshape(-1), cond_b_grad.reshape(-1)
    else:
        bias = pair_bias(pair_features, pair_w)
        keyval = lax.all_gather(keyval_own, "seq", axis=0, tiled=False)
        attend, probs = token_attention(queries, keyval, bias)
        sig_gate = jax.nn.sigmoid(gating)
        gated_low = (attend * sig_gate).astype(bf16)
        branch = dot_last(gated_low, out_w)
        gate_one = jax.nn.sigmoid(parts[2])
        mid = block_in + gate_one * branch
        normed_mid, inv_mid = norm_stats(mid)
        scale_two = jax.nn.sigmoid(parts[3])
        ffn_in = (scale_two * normed_mid + parts[4]).astype(bf16)
        upper = dot_last(ffn_in, up_w)
        hidden_width = down_w.shape[0]
        first_half, second_half = upper[..., :hidden_width], upper[..., hidden_width:]
        sig_first = jax.nn.sigmoid(first_half)
        hidden = (first_half * sig_first * second_half).astype(bf16)
        branch_two = dot_last(hidden, down_w)
        gate_two = jax.nn.sigmoid(parts[5])
        block_out = (mid + gate_two * branch_two).astype(bf16)

        out_grad = cotangent.astype(f32)
        branch_two_low = (out_grad * gate_two).astype(bf16)
        gate_two_grad = out_grad * branch_two * gate_two * (1.0 - gate_two)
        hidden_grad = dot_back(branch_two_low, down_w)
        first_grad = hidden_grad * second_half * sig_first * (1.0 + first_half * (1.0 - sig_first))
        second_grad = hidden_grad * first_half * sig_first
        upper_grad = jnp.concatenate([first_grad, second_grad], -1).astype(bf16)
        ffn_grad = dot_back(upper_grad, up_w)
        scale_two_grad = ffn_grad * normed_mid * scale_two * (1.0 - scale_two)
        mid_grad = out_grad + norm_back(normed_mid, inv_mid, ffn_grad * scale_two)
        branch_low = (mid_grad * gate_one).astype(bf16)
        gate_one_grad = mid_grad * branch * gate_one * (1.0 - gate_one)
        gated_grad = dot_back(branch_low, out_w)
        attend_low = (gated_grad * sig_gate).astype(bf16)
        gating_grad = gated_grad * attend * sig_gate * (1.0 - sig_gate)
        query_grad, keyval_part, bias_grad = token_attention_back(queries, keyval, probs, attend_low)
        keyval_grad = lax.psum_scatter(keyval_part, "seq", scatter_dimension=0, tiled=False)
        pairw_grad = pair_grad(pair_features, bias_grad, pair_w)
        mix_grad = jnp.concatenate(
            [query_grad.astype(bf16), keyval_grad, gating_grad.astype(bf16)], -1
        )
        token_qb_grad = jnp.sum(query_grad, (0, 1))
        attn_in_grad = dot_back(mix_grad, proj_w)
        scale_one = jax.nn.sigmoid(parts[0])
        scale_one_grad = attn_in_grad * normed_in * scale_one * (1.0 - scale_one)
        token_grad = mid_grad + norm_back(normed_in, inv_in, attn_in_grad * scale_one)
        cond_grad = jnp.concatenate(
            [scale_one_grad, attn_in_grad, gate_one_grad, scale_two_grad, ffn_grad, gate_two_grad], -1
        ).astype(bf16)
        cond_b_grad = jnp.sum(cond_grad.astype(f32), (0, 1))
    pairw_grad = pairw_grad.T

    if kernels:
        atom_grad, qb_grad, pairw_stack, pairw_mean, small, units = atom_backward_sum(
            token_grad,
            starts,
            stored,
            atom_input,
            pairs_t,
            share,
            wide,
            down,
            GradSum([part.shape for part in large]),
            grad_units,
        )
    else:
        mix_part, own, left, right, atom_mid_grad, *atom_totals = atom_backward(
            token_grad, starts, stored, pairs_t, share, wide, down
        )
        from_right = lax.ppermute(left, "seq", down_pairs)
        from_left = lax.ppermute(right, "seq", up_pairs)
        atom_grad, atom_proj_grad = atom_input_backward(
            atom_input, mix_part, own, from_left, from_right, atom_mid_grad, wide
        )
        qb_grad, outw_grad, upw_grad, downw_grad, pool_grad, pairw_stack, pairw_mean = atom_totals
    diagonal = pairw_stack.reshape(ATOM_HEADS, WIN_Q, WIN_Q, features)
    atom_pw_grad = (
        jnp.sum(jnp.where(eye[None, :, :, None], diagonal, 0.0), (1, 2)).T
        - jnp.sum(pairw_mean.reshape(ATOM_HEADS, -1), 1)[None, :]
    )

    rows = atom_width // samp
    tiny_parts = [qb_grad.reshape(-1), atom_pw_grad, cond_b_grad, token_qb_grad, pairw_grad]
    tiny_flat = jnp.concatenate([part.astype(bf16).reshape(samp, -1) for part in tiny_parts], 1)
    spare = atom_width
    tiny_flat = jnp.pad(tiny_flat, ((0, 0), (0, rows * spare - tiny_flat.shape[1])))
    tiny_rows = tiny_flat.reshape(samp, rows, spare)
    if kernels:
        total, units = small_sums(small, tiny_rows, units)
        *shares, pool_out, proj_out, downw_out, upw_out, outw_out, tiny_out = unpack(
            units, total, [part.shape for part in large], rows, atom_width
        )
    else:
        lanes = lambda part: part.astype(bf16).reshape(samp, rows, -1)
        downw_two = downw_grad.astype(bf16).reshape(samp, 2, rows, atom_width)
        small = jnp.stack(
            [
                lanes(pool_grad),
                jnp.concatenate([lanes(atom_proj_grad), downw_two[:, 0], downw_two[:, 1]], -1),
                jnp.concatenate([lanes(upw_grad), lanes(outw_grad), tiny_rows], -1),
                jnp.zeros((samp, rows, width), bf16),
            ],
            1,
        )
        factors = [
            (attn_in, mix_grad),
            (ffn_in, upper_grad),
            (hidden, branch_two_low),
            (cond_low, cond_grad),
            (gated_low, branch_low),
        ]
        shares, rest = sum_shares(
            [weight_grad(*pair) for pair in factors], small.reshape(-1, width)
        )
        rest = rest.reshape(-1, width)
        pool_out, second, third = rest[:rows], rest[rows : 2 * rows], rest[2 * rows : 3 * rows]
        low = 4 * atom_width
        proj_out = second[:, :low]
        downw_out = jnp.concatenate(
            [second[:, low : low + atom_width], second[:, low + atom_width :]], 0
        )
        upw_out, outw_out = third[:, :low], third[:, low : low + atom_width]
        tiny_out = third[:, low + atom_width :]
    tiny_out = tiny_out.reshape(-1)
    tiny_shares, cut = [], 0
    for part in tiny_parts:
        size = part.size // samp
        shape = (part.shape[0] // samp,) + part.shape[1:]
        tiny_shares.append(tiny_out[cut : cut + size].reshape(shape))
        cut += size
    return (
        block_out,
        atom_grad,
        token_grad,
        proj_out,
        tiny_shares[0],
        tiny_shares[1],
        outw_out,
        upw_out,
        downw_out,
        pool_out,
        shares[3],
        tiny_shares[2],
        shares[0],
        tiny_shares[3],
        tiny_shares[4],
        shares[4],
        shares[1],
        shares[2],
    )


def solution(mesh):
    in_specs = (
        P("samp", "seq", None),
        P("samp", "seq", None),
        P(),
        P("seq"),
        P("seq", None, None, None),
        P("seq", None, None),
        P("seq", None),
        P("samp"),
        P(),
        P("samp", None),
        P("samp"),
        P("samp", None),
        P("samp", None),
        P("samp", None),
        P("samp", None),
        P("samp", None),
        P("samp", None),
        P("samp"),
        P("samp", None),
        P("samp"),
        P("samp", None),
        P("samp", None),
        P("samp", None),
        P("samp", None),
        P("samp", "seq", None),
    )
    out_specs = (
        P("samp", "seq", None),
        P("samp", "seq", None),
        P("samp", "seq", None),
        P("samp", None),
        P("samp"),
        P("samp", None),
        P("samp", None),
        P("samp", None),
        P("samp", None),
        P("samp", None),
        P("samp", None),
        P("samp"),
        P("samp", None),
        P("samp"),
        P("samp", None),
        P("samp", None),
        P("samp", None),
        P("samp", None),
    )
    return jax.shard_map(local, mesh=mesh, in_specs=in_specs, out_specs=out_specs, check_vma=False)
```

profile of v0, /device:TPU:0, one launch (start us, length us, event | category | flops | bytes accessed | tf_op | source)
XLA Modules:
  0.0 458.6 jit_solution(2913969075729572974)
XLA Ops:
  0.7 0.8 pad_dynamic-slice_fusion
  1.4 1.2 add_add_fusion.starts
  2.7 0.8 reshape.208
  3.4 1.2 reshape.207.direction_ref
  4.7 0.8 copy.45
  5.5 0.1 reshape.209
  5.5 2.1 concatenate.6
  7.7 0.6 pad_bitcast_fusion.1.tiny_ref
  8.4 0.1 broadcast_in_dim.66
  8.7 0.8 broadcast_in_dim.67.share_ref
  9.5 0.9 broadcast_in_dim.65.blocked_ref
  10.4 16.1 %edges.1 = (bf16[128,1920]{1,0:T(8,128)(2,1)}, bf16[256,128]{1,0:T(8,128)(2,1)}, bf16[64,128]{1,0:T(8,128)(2,1)}, bf16[8,704,128]{2,1,0:T(8,128)(2,1)}) custom-call(bf16[32,512]{1,0:T(8,128)(2,1)} %proj_ref.1, bf16[32,512]{1,0:T(8,128)(2,1)} %upw_ref.1, bf16[32,768]{1,0:T(8,128)(2,1)} %pool_ref.1, bf16[32,128]{1,0:T(8,128)(2,1)} %outw_ref.1, ...), custom_call_target="tpu_custom_call" | custom-call | tf_op jit(solution)/shard_map/edges/pallas_call | solution.py:500
  26.5 0.7 reshape.212
  27.4 0.6 reshape.230.qbias_ref
  28.2 0.7 reshape.232.qbias_ref
  28.9 0.6 copy.51
  29.6 0.7 copy.47
  30.3 0.3 broadcast_select_fusion
  30.6 0.3 select_n.27
  30.9 0.8 copy.46.spread_ref
  31.6 87.2 %atom_forward.1 = (f32[8,64,768]{2,1,0:T(8,128)}, bf16[8,512,128]{2,1,0:T(8,128)(2,1)}, bf16[8,704,256]{2,1,0:T(8,128)(2,1)}, f32[8,512,128]{2,1,0:T(8,128)}, bf...) custom-call(s32[16]{0:T(128)} %add_add_fusion.starts, ...), custom_call_target="tpu_custom_call" | custom-call | tf_op jit(solution)/shard_map/atom_forward/pallas_call | solution.py:1080
  118.9 11.7 %token_open.1 = (f32[512,768]{1,0:T(8,128)}, bf16[512,384]{1,0:T(8,128)(2,1)}, f32[512,4608]{1,0:T(8,128)}, bf16[512,768]{1,0:T(8,128)(2,1)}, bf16[512,768]{1,0:...) custom-call(f32[8]{0:T(128)} %noise.1, f32[1,384]{1,0:T(1,128)} %reshape.207.direction_ref, ...), custom_call_target="tpu_custom_call" | custom-call | tf_op jit(solution)/shard_map/token_open/pallas_call | solution.py:1921
  130.6 79.0 %gather_attend.1 = (bf16[8,16,64,512]{3,2,1,0:T(8,128)(2,1)}, bf16[8,8,64,1536]{3,2,1,0:T(8,128)(2,1)}, f32[2,8,8,512]{3,2,1,0:T(8,128)}, bf16[512,768]{1,0:T(8,...) custom-call(bf16[8,64,768]{2,1,0:T(8,128)(2,1)} %bitcast.37, ...), custom_call_target="tpu_custom_call" | custom-call | tf_op jit(solution)/shard_map/gather_attend/pallas_call | solution.py:2211
  209.7 65.9 %attend_back_scatter.1 = (f32[8,64,768]{2,1,0:T(8,128)}, bf16[8,64,1536]{2,1,0:T(8,128)(2,1)}, f32[16,128]{1,0:T(8,128)}, f32[16,512]{1,0:T(8,128)}, bf16[768,30...) custom-call(bf16[8,64,768]{2,1,0:T(8,128)(2,1)} %bitcast.38, ...), custom_call_target="tpu_custom_call" | custom-call | tf_op jit(solution)/shard_map/attend_back_scatter/pallas_call | solution.py:2471
  275.6 26.9 %token_close.1 = (f32[512,768]{1,0:T(8,128)}, f32[1,768]{1,0:T(1,128)}, f32[1,4608]{1,0:T(1,128)}, bf16[8,4,336,768]{3,2,1,0:T(8,128)(2,1)}) custom-call(f32[512,768]{1,0:T(8,128)} %bitcast.41, bf16[512,1536]{1,0:T(8,128)(2,1)} %bitcast.42, bf16[512,768]{1,0:T(8,128)(2,1)} %get-tuple-element.113.gategrad_ref, f32[512,768]{1,0:T(8,128)} %get-tuple-element.114.midgrad_ref, ...), custom_call_target="tpu_custom_call" | custom-call | tf_op jit(solution)/shard_map/token_close/pallas_call | solution.py:2631
  302.6 109.9 %atom_backward.1 = (f32[8,512,128]{2,1,0:T(8,128)}, f32[1,128]{1,0:T(1,128)}, f32[128,512]{1,0:T(8,128)}, f32[128,128]{1,0:T(8,128)}, bf16[4,128,768]{2,1,0:T(8,128)(2,1)}, /*index=5*/bf16[8,336,768]{2,1,0:T(8,128)(2,1)}) custom-call(s32[16]{0:T(128)} %add_add_fusion.starts, f32[8,64,768]{2,1,0:T(8,128)} %bitcast.39, ...), custom_call_target="tpu_custom_call" | custom-call | tf_op jit(solution)/shard_map/atom_backward/pallas_call | solution.py:1481
  412.4 0.6 convert_reduce_fusion.2
  413.1 0.9 reduce_sum.35
  414.1 0.1 reduce_sum.38
  414.4 0.1 reduce_sum.37
  414.7 0.1 copy.49
  414.8 0.1 reshape.227
  414.9 1.1 copy.48
  416.0 0.4 reshape.225
  416.5 0.6 select_reduce_fusion
  417.1 0.1 concatenate.7
  417.3 0.6 copy.54
  417.9 23.4 %small_sums.1 = (bf16[128,768]{1,0:T(8,128)(2,1)}, bf16[8,336,768]{2,1,0:T(8,128)(2,1)}) custom-call(bf16[4,128,768]{2,1,0:T(8,128)(2,1)} %get-tuple-element.130.main, bf16[4,32,128]{2,1,0:T(8,128)(2,1)} %bitcast.49, bf16[8,336,768]{2,1,0:T(8,128)(2,1)} %get-tuple-element.138.own), custom_call_target="tpu_custom_call" | custom-call | tf_op jit(solution)/shard_map/small_sums/pallas_call | solution.py:886
  441.3 7.7 %unpack.1 = (f32[192,3072]{1,0:T(8,128)}, f32[192,3072]{1,0:T(8,128)}, f32[384,768]{1,0:T(8,128)}, f32[96,4608]{1,0:T(8,128)}, f32[192,768]{1,0:T(8,128)}, /*ind...) custom-call(bf16[8,336,768]{2,1,0:T(8,128)(2,1)} %get-tuple-element., ...), custom_call_target="tpu_custom_call" | custom-call | tf_op jit(solution)/shard_map/unpack/pallas_call | solution.py:1571
  449.0 1.3 slice.62
  450.4 1.3 slice.65
  451.7 1.4 slice.64
  453.1 0.8 slice.54
  453.9 0.7 copy.50
  454.6 1.2 slice.50
  455.8 0.6 slice.63
  456.4 0.9 copy.57
  457.3 1.3 copy.58
  (36 shorter events, 1.5 us)
Async XLA Ops:
  302.5 111.6 %copy-start.2 = (f32[16,512]{1,0:T(8,128)S(1)}, f32[16,512]{1,0:T(8,128)}, u32[]{:S(2)}) copy-start(f32[16,512]{1,0:T(8,128)} %get-tuple-element.137) | copy-start | bytes 98308
  302.5 111.7 %copy-start.4 = (f32[16,128]{1,0:T(8,128)S(1)}, f32[16,128]{1,0:T(8,128)}, u32[]{:S(2)}) copy-start(f32[16,128]{1,0:T(8,128)} %get-tuple-element.136) | copy-start | bytes 24580
  302.6 112.0 %copy-start.5 = (f32[1,768]{1,0:T(1,128)S(1)}, f32[1,768]{1,0:T(1,128)}, u32[]{:S(2)}) copy-start(f32[1,768]{1,0:T(1,128)} %get-tuple-element.135) | copy-start | bytes 9220
  302.6 112.1 %copy-start.3 = (f32[1,4608]{1,0:T(1,128)S(1)}, f32[1,4608]{1,0:T(1,128)}, u32[]{:S(2)}) copy-start(f32[1,4608]{1,0:T(1,128)} %get-tuple-element.134) | copy-start | bytes 55300
  441.3 15.1 %copy-start.1 = (bf16[512,768]{1,0:T(8,128)(2,1)S(1)}, bf16[512,768]{1,0:T(8,128)(2,1)}, u32[]{:S(2)}) copy-start(bf16[512,768]{1,0:T(8,128)(2,1)} %get-tuple-element.100) | copy-start | bytes 2359300
  449.0 8.3 %copy-start = (f32[8,512,128]{2,1,0:T(8,128)S(1)}, f32[8,512,128]{2,1,0:T(8,128)}, u32[]{:S(2)}) copy-start(f32[8,512,128]{2,1,0:T(8,128)} %get-tuple-element.189) | copy-start | bytes 6291460
where the time goes:
time: 460 us; the launch traced here: 459 us
  Pallas kernels  428 us (93%)
  local copies, waits for them, and re-layouts  25.4 us (6%)
    pallas_call x1, Pallas kernels, atom_backward_sum(): pl.pallas_call(functools.partial(atom_bwd_sum_kernel, summing), out_shape...  110 us
    pallas_call x1, Pallas kernels, atom_forward(): pl.pallas_call(functools.partial(atom_fwd_kernel, gather), out_shape=[jax...  87.2 us
    pallas_call x1, Pallas kernels, gather_attend(): pl.pallas_call(gather_attend_kernel, out_shape=[jax.ShapeDtypeStruct((sam...  79 us
    pallas_call x1, Pallas kernels, attend_back_scatter(): pl.pallas_call(attend_back_scatter_kernel, out_shape=[jax.ShapeDtypeStruc...  65.9 us
    pallas_call x1, Pallas kernels, token_close(): pl.pallas_call(token_close_kernel, out_shape=[jax.ShapeDtypeStruct((rows,...  26.9 us
    pallas_call x1, Pallas kernels, small_sums(): pl.pallas_call(small_sum_kernel, out_shape=[jax.ShapeDtypeStruct((seq * r...  23.4 us
    pallas_call x1, Pallas kernels, edges(): pl.pallas_call(functools.partial(edge_kernel, samp, seq), out_shape=[jax....  16.1 us
    pallas_call x1, Pallas kernels, token_open(): pl.pallas_call(token_open_kernel, out_shape=[jax.ShapeDtypeStruct((rows,...  11.7 us

commit v1 on v0

--- a/solution.py
+++ b/solution.py
@@ -1906,7 +1906,7 @@
 def token_open(noise, direction, single, pooled, tokens, condw, condb, proj, qbias):
     samples, count, width = tokens.shape
     rows = samples * count
-    block = 2 * count
+    block = 4 * count
     lanes = lambda size: pl.BlockSpec((block, size), lambda i: (i, 0))
     inner = single.shape[1]
     outs = (
@@ -2618,7 +2618,7 @@
 def token_close(dq, dkv, gategrad, midgrad, block_in, cond_all, tail, proj, attn_in, cond_low, ready, samp, seq):
     samples, tokens, width = dq.shape
     rows = samples * tokens
-    blocks = 4
+    blocks = 2
     block = rows // blocks
     flat = lambda part: part.reshape(rows, part.shape[-1])
     upw, downw, outw = ready

time: 460 us -> 457 us (level)
  no operation moved by 1% of the time
where the time goes in v1:
time: 457 us; the launch traced here: 456 us
  Pallas kernels  425 us (93%)
  local copies, waits for them, and re-layouts  25.4 us (6%)
    pallas_call x1, Pallas kernels, atom_backward_sum(): pl.pallas_call(functools.partial(atom_bwd_sum_kernel, summing), out_shape...  110 us
    pallas_call x1, Pallas kernels, atom_forward(): pl.pallas_call(functools.partial(atom_fwd_kernel, gather), out_shape=[jax...  87.2 us
    pallas_call x1, Pallas kernels, gather_attend(): pl.pallas_call(gather_attend_kernel, out_shape=[jax.ShapeDtypeStruct((sam...  79 us
    pallas_call x1, Pallas kernels, attend_back_scatter(): pl.pallas_call(attend_back_scatter_kernel, out_shape=[jax.ShapeDtypeStruc...  65.9 us
    pallas_call x1, Pallas kernels, token_close(): pl.pallas_call(token_close_kernel, out_shape=[jax.ShapeDtypeStruct((rows,...  24.4 us
    pallas_call x1, Pallas kernels, small_sums(): pl.pallas_call(small_sum_kernel, out_shape=[jax.ShapeDtypeStruct((seq * r...  23.4 us
    pallas_call x1, Pallas kernels, edges(): pl.pallas_call(functools.partial(edge_kernel, samp, seq), out_shape=[jax....  16.1 us
    pallas_call x1, Pallas kernels, token_open(): pl.pallas_call(token_open_kernel, out_shape=[jax.ShapeDtypeStruct((rows,...  11.1 us

profile of v1, /device:TPU:0, one launch (start us, length us, event | category | flops | bytes accessed | tf_op | source)
XLA Modules:
  0.0 455.5 jit_solution(6919917632426628216)
XLA Ops:
  0.7 0.8 pad_dynamic-slice_fusion
  1.4 1.2 add_add_fusion.starts
  2.7 0.8 reshape.208
  3.4 1.2 reshape.207.direction_ref
  4.7 0.8 copy.45
  5.5 0.1 reshape.209
  5.5 2.1 concatenate.6
  7.7 0.6 pad_bitcast_fusion.1.tiny_ref
  8.4 0.1 broadcast_in_dim.66
  8.7 0.8 broadcast_in_dim.67.share_ref
  9.5 0.9 broadcast_in_dim.65.blocked_ref
  10.4 16.1 %edges.1 = (bf16[128,1920]{1,0:T(8,128)(2,1)}, bf16[256,128]{1,0:T(8,128)(2,1)}, bf16[64,128]{1,0:T(8,128)(2,1)}, bf16[8,704,128]{2,1,0:T(8,128)(2,1)}) custom-call(bf16[32,512]{1,0:T(8,128)(2,1)} %proj_ref.1, bf16[32,512]{1,0:T(8,128)(2,1)} %upw_ref.1, bf16[32,768]{1,0:T(8,128)(2,1)} %pool_ref.1, bf16[32,128]{1,0:T(8,128)(2,1)} %outw_ref.1, ...), custom_call_target="tpu_custom_call" | custom-call | tf_op jit(solution)/shard_map/edges/pallas_call | solution.py:500
  26.5 0.7 reshape.212
  27.4 0.6 reshape.230.qbias_ref
  28.2 0.7 reshape.232.qbias_ref
  28.9 0.6 copy.51
  29.6 0.7 copy.47
  30.3 0.3 broadcast_select_fusion
  30.6 0.3 select_n.27
  30.9 0.8 copy.46.spread_ref
  31.6 87.2 %atom_forward.1 = (f32[8,64,768]{2,1,0:T(8,128)}, bf16[8,512,128]{2,1,0:T(8,128)(2,1)}, bf16[8,704,256]{2,1,0:T(8,128)(2,1)}, f32[8,512,128]{2,1,0:T(8,128)}, bf...) custom-call(s32[16]{0:T(128)} %add_add_fusion.starts, ...), custom_call_target="tpu_custom_call" | custom-call | tf_op jit(solution)/shard_map/atom_forward/pallas_call | solution.py:1080
  118.9 11.1 %token_open.1 = (f32[512,768]{1,0:T(8,128)}, bf16[512,384]{1,0:T(8,128)(2,1)}, f32[512,4608]{1,0:T(8,128)}, bf16[512,768]{1,0:T(8,128)(2,1)}, bf16[512,768]{1,0:...) custom-call(f32[8]{0:T(128)} %noise.1, f32[1,384]{1,0:T(1,128)} %reshape.207.direction_ref, ...), custom_call_target="tpu_custom_call" | custom-call | tf_op jit(solution)/shard_map/token_open/pallas_call | solution.py:1921
  130.0 79.0 %gather_attend.1 = (bf16[8,16,64,512]{3,2,1,0:T(8,128)(2,1)}, bf16[8,8,64,1536]{3,2,1,0:T(8,128)(2,1)}, f32[2,8,8,512]{3,2,1,0:T(8,128)}, bf16[512,768]{1,0:T(8,...) custom-call(bf16[8,64,768]{2,1,0:T(8,128)(2,1)} %bitcast.37, ...), custom_call_target="tpu_custom_call" | custom-call | tf_op jit(solution)/shard_map/gather_attend/pallas_call | solution.py:2211
  209.1 65.9 %attend_back_scatter.1 = (f32[8,64,768]{2,1,0:T(8,128)}, bf16[8,64,1536]{2,1,0:T(8,128)(2,1)}, f32[16,128]{1,0:T(8,128)}, f32[16,512]{1,0:T(8,128)}, bf16[768,30...) custom-call(bf16[8,64,768]{2,1,0:T(8,128)(2,1)} %bitcast.38, ...), custom_call_target="tpu_custom_call" | custom-call | tf_op jit(solution)/shard_map/attend_back_scatter/pallas_call | solution.py:2471
  275.0 24.4 %token_close.1 = (f32[512,768]{1,0:T(8,128)}, f32[1,768]{1,0:T(1,128)}, f32[1,4608]{1,0:T(1,128)}, bf16[8,4,336,768]{3,2,1,0:T(8,128)(2,1)}) custom-call(f32[512,768]{1,0:T(8,128)} %bitcast.41, bf16[512,1536]{1,0:T(8,128)(2,1)} %bitcast.42, bf16[512,768]{1,0:T(8,128)(2,1)} %get-tuple-element.113.gategrad_ref, f32[512,768]{1,0:T(8,128)} %get-tuple-element.114.midgrad_ref, ...), custom_call_target="tpu_custom_call" | custom-call | tf_op jit(solution)/shard_map/token_close/pallas_call | solution.py:2631
  299.5 109.9 %atom_backward.1 = (f32[8,512,128]{2,1,0:T(8,128)}, f32[1,128]{1,0:T(1,128)}, f32[128,512]{1,0:T(8,128)}, f32[128,128]{1,0:T(8,128)}, bf16[4,128,768]{2,1,0:T(8,128)(2,1)}, /*index=5*/bf16[8,336,768]{2,1,0:T(8,128)(2,1)}) custom-call(s32[16]{0:T(128)} %add_add_fusion.starts, f32[8,64,768]{2,1,0:T(8,128)} %bitcast.39, ...), custom_call_target="tpu_custom_call" | custom-call | tf_op jit(solution)/shard_map/atom_backward/pallas_call | solution.py:1481
  409.3 0.6 convert_reduce_fusion.2
  410.0 0.9 reduce_sum.35
  411.0 0.1 reduce_sum.38
  411.3 0.1 reduce_sum.37
  411.6 0.1 copy.49
  411.7 0.1 reshape.227
  411.8 1.1 copy.48
  412.9 0.4 reshape.225
  413.4 0.6 select_reduce_fusion
  414.0 0.1 concatenate.7
  414.2 0.6 copy.54
  414.8 23.4 %small_sums.1 = (bf16[128,768]{1,0:T(8,128)(2,1)}, bf16[8,336,768]{2,1,0:T(8,128)(2,1)}) custom-call(bf16[4,128,768]{2,1,0:T(8,128)(2,1)} %get-tuple-element.130.main, bf16[4,32,128]{2,1,0:T(8,128)(2,1)} %bitcast.49, bf16[8,336,768]{2,1,0:T(8,128)(2,1)} %get-tuple-element.138.own), custom_call_target="tpu_custom_call" | custom-call | tf_op jit(solution)/shard_map/small_sums/pallas_call | solution.py:886
  438.2 7.7 %unpack.1 = (f32[192,3072]{1,0:T(8,128)}, f32[192,3072]{1,0:T(8,128)}, f32[384,768]{1,0:T(8,128)}, f32[96,4608]{1,0:T(8,128)}, f32[192,768]{1,0:T(8,128)}, /*ind...) custom-call(bf16[8,336,768]{2,1,0:T(8,128)(2,1)} %get-tuple-element., ...), custom_call_target="tpu_custom_call" | custom-call | tf_op jit(solution)/shard_map/unpack/pallas_call | solution.py:1571
  445.9 1.3 slice.62
  447.3 1.3 slice.65
  448.6 1.4 slice.64
  450.0 0.8 slice.54
  450.8 0.7 copy.50
  451.5 1.2 slice.50
  452.7 0.6 slice.63
  453.3 0.9 copy.57
  454.2 1.3 copy.58
  (36 shorter events, 1.5 us)
Async XLA Ops:
  299.4 111.6 %copy-start.2 = (f32[16,512]{1,0:T(8,128)S(1)}, f32[16,512]{1,0:T(8,128)}, u32[]{:S(2)}) copy-start(f32[16,512]{1,0:T(8,128)} %get-tuple-element.137) | copy-start | bytes 98308
  299.4 111.7 %copy-start.4 = (f32[16,128]{1,0:T(8,128)S(1)}, f32[16,128]{1,0:T(8,128)}, u32[]{:S(2)}) copy-start(f32[16,128]{1,0:T(8,128)} %get-tuple-element.136) | copy-start | bytes 24580
  299.5 111.9 %copy-start.5 = (f32[1,768]{1,0:T(1,128)S(1)}, f32[1,768]{1,0:T(1,128)}, u32[]{:S(2)}) copy-start(f32[1,768]{1,0:T(1,128)} %get-tuple-element.135) | copy-start | bytes 9220
  299.5 112.1 %copy-start.3 = (f32[1,4608]{1,0:T(1,128)S(1)}, f32[1,4608]{1,0:T(1,128)}, u32[]{:S(2)}) copy-start(f32[1,4608]{1,0:T(1,128)} %get-tuple-element.134) | copy-start | bytes 55300
  438.2 15.1 %copy-start.1 = (bf16[512,768]{1,0:T(8,128)(2,1)S(1)}, bf16[512,768]{1,0:T(8,128)(2,1)}, u32[]{:S(2)}) copy-start(bf16[512,768]{1,0:T(8,128)(2,1)} %get-tuple-element.100) | copy-start | bytes 2359300
  445.9 8.3 %copy-start = (f32[8,512,128]{2,1,0:T(8,128)S(1)}, f32[8,512,128]{2,1,0:T(8,128)}, u32[]{:S(2)}) copy-start(f32[8,512,128]{2,1,0:T(8,128)} %get-tuple-element.189) | copy-start | bytes 6291460
